TPU v7x, 32 devices: a whole 2x2x4 slice. The times are simulated.
32 devices in a mesh: segment: 2 (over x), dp: 4 (over z), mp: 4 (over y, core).
Axes of the slice: x: 2, y: 2, z: 4, core: 2. Of those that a mesh axis runs over, the one named last changes fastest.
Arguments:
- patch_tokens: bfloat16 [32, 16, 3072], P('dp', None, 'mp'), may hold values from -400 to 400
- visible_index: int32 [32, 16], P('dp'), may hold values from 0 to 63, as said below
- output_grad: bfloat16 [32, 16, 3072], P('dp', None, 'mp'), may hold values from -1.5 to 1.5
- norm_gain: float32 [2, 3072], P('segment'), may hold values from 0.1 to 1.9
- master_weights: float32 [2, 12288, 2048], P('segment', 'dp', 'mp'), may hold values from -2 to 2
- first_moment: float32 [2, 12288, 2048], P('segment', 'dp', 'mp'), may hold values from -6 to 6
- second_moment: float32 [2, 12288, 2048], P('segment', 'dp', 'mp'), may hold values from 0.01 to 1
Outputs:
- new_master: float32 [2, 12288, 2048], P('segment', 'dp', 'mp')
- new_first: float32 [2, 12288, 2048], P('segment', 'dp', 'mp')
- new_second: float32 [2, 12288, 2048], P('segment', 'dp', 'mp')
Inputs may be any that keep to these rules, and one draw needn't show every extreme that they name: `visible_index`: in each volume the 16 indices are distinct and increasing.
All inputs are finite; a program needn't handle non-finite values.
Results may differ from a plain program's by a relative error of at most 0.02.
Values may be sent and summed in bfloat16 or wider, within the bound.
A program may use at most 192 MiB of HBM per device.

v0:
```python
import math

import jax
import jax.numpy as jnp
from jax import lax
from jax.sharding import PartitionSpec as P

HD = 128
MB_VOLS = 2


beta_one = 0.9
beta_two = 0.95
learn_rate = 0.01
decay_rate = 0.1
adam_eps = 1e-08
norm_eps = 1e-05
step_count = 10


def from_behind(array, axis, by):
    peers = lax.axis_size(axis)
    pairs = [(i, i + by) for i in range(peers) if 0 <= i + by < peers]
    return lax.ppermute(array, axis, pairs)


def position_table(visible_index, model_width):
    half_width = model_width // 2
    angle_rate = jnp.exp(
        jnp.arange(half_width, dtype=jnp.float32) * (-2.0 * math.log(10000.0) / model_width)
    )
    angles = visible_index.astype(jnp.float32)[..., None] * angle_rate
    return jnp.concatenate([jnp.sin(angles), jnp.cos(angles)], axis=-1)


def norm_forward(hidden, norm_scale):
    values = hidden.astype(jnp.float32)
    centred = values - jnp.mean(values, axis=-1, keepdims=True)
    inverse_dev = lax.rsqrt(jnp.mean(centred * centred, axis=-1, keepdims=True) + norm_eps)
    standard = centred * inverse_dev
    return ((standard * norm_scale).astype(jnp.bfloat16), standard, inverse_dev)


def norm_backward(d_normed, d_output, standard, inverse_dev, norm_scale):
    scaled = d_normed * norm_scale
    inner = (
        scaled
        - jnp.mean(scaled, axis=-1, keepdims=True)
        - standard * jnp.mean(scaled * standard, axis=-1, keepdims=True)
    )
    return (d_output.astype(jnp.float32) + inner * inverse_dev).astype(jnp.bfloat16)


def softmax_rows(scores):
    lifted = jnp.exp(scores - jnp.max(scores, axis=-1, keepdims=True))
    return lifted / jnp.sum(lifted, axis=-1, keepdims=True)


def rounded(values):
    return lax.optimization_barrier(values.astype(jnp.bfloat16)).astype(jnp.float32)


def adam_update(gradient, master, first_moment, second_moment):
    new_first = beta_one * first_moment + (1.0 - beta_one) * gradient
    new_second = beta_two * second_moment + (1.0 - beta_two) * gradient * gradient
    direction = (
        new_first
        / (1.0 - beta_one**step_count)
        / (jnp.sqrt(new_second / (1.0 - beta_two**step_count)) + adam_eps)
    )
    new_master = master - learn_rate * (direction + decay_rate * master)
    return (new_master, new_first, new_second)


def layer_local(layer_in, norm_scale, weights):
    row_count, model_width = layer_in.shape
    col_count = weights.shape[1]
    head_count = col_count // HD
    length = row_count // MB_VOLS
    normed, standard, inverse_dev = norm_forward(layer_in, norm_scale)
    triple = weights[: 3 * model_width].reshape(3, model_width, col_count)
    project = jnp.einsum("nd,sdc->nsc", normed, triple, preferred_element_type=jnp.float32).astype(
        jnp.bfloat16
    )
    shaped = project.reshape(MB_VOLS, length, 3, head_count, HD)
    scores = jnp.einsum(
        "vqhe,vkhe->vhqk", shaped[:, :, 0], shaped[:, :, 1], preferred_element_type=jnp.float32
    ) * (1.0 / math.sqrt(HD))
    softmaxed = softmax_rows(scores)
    probs_half = softmaxed.astype(jnp.bfloat16)
    attended = jnp.einsum(
        "vhqk,vkhe->vqhe", probs_half, shaped[:, :, 2], preferred_element_type=jnp.float32
    )
    attended = attended.astype(jnp.bfloat16).reshape(row_count, col_count)
    return (normed, standard, inverse_dev, project, softmaxed, probs_half, attended)


def head_terms(attended, weights, model_width):
    return rounded(
        jnp.einsum(
            "nc,dc->nd", attended, weights[3 * model_width :], preferred_element_type=jnp.float32
        )
    )


def attention_back(d_output, saved_vals, weights):
    project, softmaxed, probs_half = (saved_vals[3], saved_vals[4], saved_vals[5])
    row_count, model_width = d_output.shape
    col_count = weights.shape[1]
    head_count = col_count // HD
    length = row_count // MB_VOLS
    shaped = project.reshape(MB_VOLS, length, 3, head_count, HD)
    d_attended = jnp.einsum(
        "nd,dc->nc", d_output, weights[3 * model_width :], preferred_element_type=jnp.float32
    )
    d_attended = d_attended.astype(jnp.bfloat16).reshape(MB_VOLS, length, head_count, HD)
    d_probs = jnp.einsum(
        "vqhe,vkhe->vhqk", d_attended, shaped[:, :, 2], preferred_element_type=jnp.float32
    )
    d_scores = (
        softmaxed
        * (d_probs - jnp.sum(d_probs * softmaxed, axis=-1, keepdims=True))
        * (1.0 / math.sqrt(HD))
    ).astype(jnp.bfloat16)
    d_queries = jnp.einsum(
        "vhqk,vkhe->vqhe", d_scores, shaped[:, :, 1], preferred_element_type=jnp.float32
    ).astype(jnp.bfloat16)
    d_keys = jnp.einsum(
        "vhqk,vqhe->vkhe", d_scores, shaped[:, :, 0], preferred_element_type=jnp.float32
    ).astype(jnp.bfloat16)
    d_values = jnp.einsum(
        "vhqk,vqhe->vkhe", probs_half, d_attended, preferred_element_type=jnp.float32
    ).astype(jnp.bfloat16)
    return jnp.stack([d_queries, d_keys, d_values], axis=2).reshape(row_count, 3, col_count)


def feature_terms(d_project, weights, model_width):
    col_count = weights.shape[1]
    triple = weights[: 3 * model_width].reshape(3, model_width, col_count)
    return rounded(jnp.einsum("nsc,sdc->nd", d_project, triple, preferred_element_type=jnp.float32))


def shards(
    patch_tokens, visible_index, output_grad, norm_gain, master_weights, first_moment, second_moment
):
    model_width = patch_tokens.shape[2] * lax.axis_size("mp")
    rows_here = master_weights.shape[1]
    is_first = lax.axis_index("segment") == 0
    norm_scale = norm_gain[0]
    weights = lax.all_gather(master_weights[0].astype(jnp.bfloat16), "dp", axis=0, tiled=True)
    tokens_full, grads_full = (
        lax.all_gather(patch_tokens, "mp", axis=2, tiled=True),
        lax.all_gather(output_grad, "mp", axis=2, tiled=True),
    )
    vol_count, length = visible_index.shape
    micro_count = vol_count // MB_VOLS
    mb_rows = MB_VOLS * length
    first_inputs = (
        tokens_full.astype(jnp.float32) + position_table(visible_index, model_width)
    ).astype(jnp.bfloat16)
    first_inputs = first_inputs.reshape(micro_count, mb_rows, model_width)
    out_grads = grads_full.reshape(micro_count, mb_rows, model_width)
    zeros_full = jnp.zeros((mb_rows, model_width), jnp.bfloat16)
    saved_ticks = []
    received = zeros_full
    for step_index in range(micro_count + 1):
        arriving = received
        own_input = first_inputs[step_index] if step_index < micro_count else zeros_full
        layer_in = jnp.where(is_first, own_input, arriving)
        saved_vals = layer_local(layer_in, norm_scale, weights)
        saved_ticks.append(saved_vals)
        if step_index < micro_count:
            head_part = head_terms(saved_vals[6], weights, model_width)
            mixed = lax.psum(head_part.astype(jnp.bfloat16), "mp").astype(jnp.float32)
            layer_out = (layer_in.astype(jnp.float32) + mixed).astype(jnp.bfloat16)
            received = from_behind(layer_out, "segment", 1)
    back_ticks = []
    for step_index in range(micro_count + 1):
        arriving = received if step_index > 0 else zeros_full
        own_grad = (
            out_grads[micro_count - 1 - step_index] if step_index < micro_count else zeros_full
        )
        d_output = jnp.where(is_first, arriving, own_grad)
        saved_vals = saved_ticks[micro_count - step_index]
        d_project = attention_back(d_output, saved_vals, weights)
        back_ticks.append((d_output, d_project))
        if step_index < micro_count:
            d_terms = feature_terms(d_project, weights, model_width)
            standard, inverse_dev = (saved_vals[1], saved_vals[2])
            summed = lax.psum(d_terms.astype(jnp.bfloat16), "mp").astype(jnp.float32)
            d_input = norm_backward(summed, d_output, standard, inverse_dev, norm_scale)
            received = from_behind(d_input, "segment", -1)
    all_steps = range(micro_count + 1)
    normed_ticks = jnp.stack([saved_ticks[micro_count - step_index][0] for step_index in all_steps])
    attended_ticks = jnp.stack(
        [saved_ticks[micro_count - step_index][6] for step_index in all_steps]
    )
    d_output_ticks = jnp.stack([back_ticks[step_index][0] for step_index in all_steps])
    d_project_ticks = jnp.stack([back_ticks[step_index][1] for step_index in all_steps])
    right_ticks = jnp.concatenate([d_project_ticks, attended_ticks[:, :, None]], axis=2)

    def pick_valid(ticks):
        chosen = jnp.where(is_first, ticks[1:], ticks[:-1])
        return chosen.reshape((micro_count * mb_rows,) + ticks.shape[2:])

    normed_all = pick_valid(normed_ticks)
    d_output_all = pick_valid(d_output_ticks)
    right_all = pick_valid(right_ticks)

    def one_piece(piece_index):
        first_row = piece_index * rows_here
        part_index = first_row // model_width
        col_offset = first_row % model_width
        left_norm = lax.dynamic_slice_in_dim(normed_all, col_offset, rows_here, 1)
        left_grad = lax.dynamic_slice_in_dim(d_output_all, col_offset, rows_here, 1)
        left_side = jnp.where(part_index == 3, left_grad, left_norm)
        right_side = lax.dynamic_index_in_dim(right_all, part_index, 1, keepdims=False)
        return jnp.einsum("tr,tc->rc", left_side, right_side, preferred_element_type=jnp.float32)

    blocks = lax.map(
        one_piece, jnp.arange(rows_here * lax.axis_size("dp") // rows_here, dtype=jnp.int32)
    )
    gradient = lax.psum_scatter(
        blocks.reshape(rows_here * lax.axis_size("dp"), blocks.shape[2]).astype(jnp.bfloat16),
        "dp",
        scatter_dimension=0,
        tiled=True,
    ).astype(jnp.float32)
    new_master, new_first, new_second = adam_update(
        gradient, master_weights[0], first_moment[0], second_moment[0]
    )
    return (new_master[None], new_first[None], new_second[None])


def solution(mesh):
    placed = (
        P("dp", None, "mp"),
        P("dp", None),
        P("dp", None, "mp"),
        P("segment", None),
        P("segment", "dp", "mp"),
        P("segment", "dp", "mp"),
        P("segment", "dp", "mp"),
    )
    return jax.shard_map(
        shards,
        mesh=mesh,
        in_specs=placed,
        out_specs=(P("segment", "dp", "mp"), P("segment", "dp", "mp"), P("segment", "dp", "mp")),
        check_vma=False,
    )
```

profile of v0, /device:TPU:0, one launch (start us, length us, event | category | flops | bytes accessed | tf_op | source)
XLA Modules:
  0.0 909.8 jit_solution(2568975783798834956)
XLA Ops:
  7.2 4.9 bitcast_convert_fusion
  12.3 10.1 %all_gather.10 = bf16[8,16,3072]{2,1,0:T(8,128)(2,1)S(1)} all-gather(bf16[8,16,768]{2,1,0:T(8,128)(2,1)S(1)} %copy-done.3), channel_id=1, replica_groups=mesh['segment'=2,'dp'=4,'mp'=4] {'mp'}, dimensions={2}, use_global_device_ids=true | all-gather | bytes 983040 | tf_op jit(solution)/shard_map/all_gather | solution.py:152
  22.3 2.8 multiply_sine_fusion
  25.8 207.5 %all-gather.2.cloned.1.call-done = bf16[12288,512]{1,0:T(8,128)(2,1)} async-done(((bf16[3072,512]{1,0:T(8,128)(2,1)}), bf16[12288,512]{1,0:T(8,128)(2,1)}) %all-gather.2.cloned.1.call-update) | async-done | bytes 12582928 | tf_op jit(solution)/shard_map/all_gather | solution.py:150
  233.2 5.2 slice.160
  238.5 3.6 copy-done
  244.9 3.6 convolution_convert_fusion.3
  248.6 30.0 %all-reduce.9.cloned.1.call-done = bf16[32,3072]{1,0:T(8,128)(2,1)} async-done(((bf16[32,3072]{1,0:T(8,128)(2,1)}), bf16[32,3072]{1,0:T(8,128)(2,1)}) %all-reduce.9.cloned.1.call-update) | async-done | bytes 196624 | tf_op jit(solution)/shard_map/psum | solution.py:174
  279.6 3.4 collective-permute-start
  283.0 3.1 collective-permute-done
  286.6 5.5 convolution_convert_fusion.7
  293.3 3.6 convolution_convert_fusion.2
  297.0 33.0 %all-reduce.11.cloned.1.call-done = bf16[32,3072]{1,0:T(8,128)(2,1)} async-done(((bf16[32,3072]{1,0:T(8,128)(2,1)}), bf16[32,3072]{1,0:T(8,128)(2,1)}) %all-reduce.11.cloned.1.call-update) | async-done | bytes 196624 | tf_op jit(solution)/shard_map/psum | solution.py:174
  330.9 3.4 collective-permute-start.1
  334.3 3.2 collective-permute-done.1
  337.9 5.5 convolution_convert_fusion.6
  344.7 3.6 convolution_convert_fusion.1
  348.4 7.8 all_gather.9
  356.2 25.1 %all-reduce.13.cloned.1.call-done = bf16[32,3072]{1,0:T(8,128)(2,1)} async-done(((bf16[32,3072]{1,0:T(8,128)(2,1)}), bf16[32,3072]{1,0:T(8,128)(2,1)}) %all-reduce.13.cloned.1.call-update) | async-done | bytes 196624 | tf_op jit(solution)/shard_map/psum | solution.py:174
  382.3 3.6 collective-permute-start.2
  386.1 2.8 collective-permute-done.2
  389.3 5.5 convolution_convert_fusion.5
  395.4 3.6 convolution_convert_fusion
  399.8 32.2 %all-reduce.15.cloned.1.call-done = bf16[32,3072]{1,0:T(8,128)(2,1)} async-done(((bf16[32,3072]{1,0:T(8,128)(2,1)}), bf16[32,3072]{1,0:T(8,128)(2,1)}) %all-reduce.15.cloned.1.call-update) | async-done | bytes 196624 | tf_op jit(solution)/shard_map/psum | solution.py:174
  433.0 3.4 collective-permute-start.3
  436.4 2.5 convolution_convert_fusion.13
  440.0 5.5 convolution_convert_fusion.4
  446.7 7.2 fusion.21
  456.2 30.7 %all-reduce.17.cloned.1.call-done = bf16[32,3072]{1,0:T(8,128)(2,1)} async-done(((bf16[32,3072]{1,0:T(8,128)(2,1)}), bf16[32,3072]{1,0:T(8,128)(2,1)}) %all-reduce.17.cloned.1.call-update) | async-done | bytes 196624 | tf_op jit(solution)/shard_map/psum | solution.py:190
  490.5 6.2 collective-permute-done.4
  496.8 2.5 convolution_convert_fusion.12
  500.4 7.2 fusion.22
  507.7 31.0 %all-reduce.19.cloned.1.call-done = bf16[32,3072]{1,0:T(8,128)(2,1)} async-done(((bf16[32,3072]{1,0:T(8,128)(2,1)}), bf16[32,3072]{1,0:T(8,128)(2,1)}) %all-reduce.19.cloned.1.call-update) | async-done | bytes 196624 | tf_op jit(solution)/shard_map/psum | solution.py:190
  542.4 6.2 collective-permute-done.5
  552.2 7.2 fusion.23
  559.6 30.9 %all-reduce.21.cloned.1.call-done = bf16[32,3072]{1,0:T(8,128)(2,1)} async-done(((bf16[32,3072]{1,0:T(8,128)(2,1)}), bf16[32,3072]{1,0:T(8,128)(2,1)}) %all-reduce.21.cloned.1.call-update) | async-done | bytes 196624 | tf_op jit(solution)/shard_map/psum | solution.py:190
  594.5 5.9 collective-permute-done.6
  600.5 2.5 convolution_convert_fusion.10
  604.1 7.2 fusion.24
  611.4 31.0 %all-reduce.23.cloned.1.call-done = bf16[32,3072]{1,0:T(8,128)(2,1)} async-done(((bf16[32,3072]{1,0:T(8,128)(2,1)}), bf16[32,3072]{1,0:T(8,128)(2,1)}) %all-reduce.23.cloned.1.call-update) | async-done | bytes 196624 | tf_op jit(solution)/shard_map/psum | solution.py:190
  646.3 6.1 collective-permute-done.7
  659.7 15.8 %while.12 = (s32[]{:T(128)}, bf16[4,3072,512]{2,1,0:T(8,128)(2,1)}, s32[4]{0:T(128)S(1)}, bf16[128,3072]{1,0:T(8,128)(2,1)S(1)}, bf16[128,3072]{1,0:T(8,128)(2,1...) while((s32[]{:T(128)}, bf16[4,3072,512]{2,1,0:T(8,128)(2,1)}, ...), condition=%wide.region_42.43_spmd, body=%wide.region_41.42_spmd.sunk | while | flops 403046400 | bytes 7996187 | solution.py:220
  661.0 2.7 bitcast_dynamic-update-slice_fusion.2
  664.9 2.7 bitcast_dynamic-update-slice_fusion.2
  668.8 2.7 bitcast_dynamic-update-slice_fusion.2
  672.8 2.7 bitcast_dynamic-update-slice_fusion.2
  675.5 211.3 %reduce-scatter.2.cloned.1.call-done = bf16[3072,512]{1,0:T(8,128)(2,1)} async-done(((bf16[12288,512]{1,0:T(8,128)(2,1)}), bf16[3072,512]{1,0:T(8,128)(2,1)}) %reduce-scatter.2.cloned.1.call-update) | async-done | bytes 3145744 | tf_op jit(solution)/shard_map/reduce_scatter | solution.py:223
  886.8 16.1 %fusion.25 = (f32[1,3072,512]{2,1,0:T(8,128)}, f32[1,3072,512]{2,1,0:T(8,128)}, f32[1,3072,512]{2,1,0:T(8,128)}) fusion(bf16[3072,512]{1,0:T(8,128)(2,1)} %reduce-scatter.2.cloned.1.call-done, f32[1,3072,512]{2,1,0:T(8,128)} %param.15, f32[1,3072,512]{2,1,0:T(8,128)} %param.14, f32[1,3072,512]{2,1,0:T(8,128)} %param.13), kind=kLoop, calls=%fused_computation.39 | loop fusion | flops 25165824 | bytes 40894464 | tf_op jit(solution)/shard_map/broadcast_in_dim | solution.py:232
  (268 shorter events, 47.9 us)
Async XLA Ops:
  7.2 5.1 copy-start.3
  7.2 226.1 %all-gather.2.cloned.1.call-start = ((), (), s32[]{:S(2)}) async-start(), calls=%async_computation.1 | async-start | bytes 15728640 | tf_op jit(solution)/shard_map/all_gather | solution.py:150
  12.1 13.5 %copy-start.1 = (f32[1,3072]{1,0:T(1,128)S(1)}, f32[1,3072]{1,0:T(1,128)}, u32[]{:S(2)}) copy-start(f32[1,3072]{1,0:T(1,128)} %param.12) | copy-start | bytes 36868
  12.2 266.4 %all-reduce.9.cloned.1.call-start = ((), (), s32[]{:S(2)}) async-start(), calls=%async_computation.2 | async-start | bytes 393216 | tf_op jit(solution)/shard_map/psum | solution.py:174
  243.7 34.8 %copy-start.17 = (bf16[2,16,1,4,128]{4,3,1,0,2:T(4,128)(2,1)}, bf16[2,16,1,4,128]{4,3,1,0,2:T(4,128)(2,1)S(1)}, u32[]{:S(2)}) copy-start(bf16[2,16,1,4,128]{4,3,1,0,2:T(4,128)(2,1)S(1)} %get-tuple-element.136) | copy-start | bytes 98308
  243.7 35.8 %copy-start.9 = (bf16[2,16,1,4,128]{4,3,1,0,2:T(4,128)(2,1)}, bf16[2,16,1,4,128]{4,3,1,0,2:T(4,128)(2,1)S(1)}, u32[]{:S(2)}) copy-start(bf16[2,16,1,4,128]{4,3,1,0,2:T(4,128)(2,1)S(1)} %get-tuple-element.137) | copy-start | bytes 98308
  243.8 35.8 %copy-start.15 = (bf16[2,16,1,4,128]{4,3,1,0,2:T(4,128)(2,1)}, bf16[2,16,1,4,128]{4,3,1,0,2:T(4,128)(2,1)S(1)}, u32[]{:S(2)}) copy-start(bf16[2,16,1,4,128]{4,3,1,0,2:T(4,128)(2,1)S(1)} %get-tuple-element.135) | copy-start | bytes 98308
  244.6 35.0 %copy-start.30 = (f32[2,4,16]{2,1,0:T(4,128)}, f32[2,4,16]{2,1,0:T(4,128)S(1)}, u32[]{:S(2)}) copy-start(f32[2,4,16]{2,1,0:T(4,128)S(1)} %get-tuple-element.140) | copy-start | bytes 1540
  248.5 81.4 %all-reduce.11.cloned.1.call-start = ((), (), s32[]{:S(2)}) async-start(), calls=%async_computation.3 | async-start | bytes 393216 | tf_op jit(solution)/shard_map/psum | solution.py:174
  279.6 6.6 collective-permute-start
  292.1 37.8 %copy-start.21 = (bf16[2,16,1,4,128]{4,3,1,0,2:T(4,128)(2,1)}, bf16[2,16,1,4,128]{4,3,1,0,2:T(4,128)(2,1)S(1)}, u32[]{:S(2)}) copy-start(bf16[2,16,1,4,128]{4,3,1,0,2:T(4,128)(2,1)S(1)} %get-tuple-element.133) | copy-start | bytes 98308
  292.9 44.7 %copy-start.32 = (f32[2,4,16]{2,1,0:T(4,128)}, f32[2,4,16]{2,1,0:T(4,128)S(1)}, u32[]{:S(2)}) copy-start(f32[2,4,16]{2,1,0:T(4,128)S(1)} %get-tuple-element.142) | copy-start | bytes 1540
  296.9 84.4 %all-reduce.13.cloned.1.call-start = ((), (), s32[]{:S(2)}) async-start(), calls=%async_computation.4 | async-start | bytes 393216 | tf_op jit(solution)/shard_map/psum | solution.py:174
  330.9 6.6 collective-permute-start.1
  337.9 10.4 %copy-start.4 = (bf16[8,16,768]{2,1,0:T(8,128)(2,1)S(1)}, bf16[8,16,768]{2,1,0:T(8,128)(2,1)}, u32[]{:S(2)}) copy-start(bf16[8,16,768]{2,1,0:T(8,128)(2,1)} %param.11) | copy-start | bytes 589828
  343.5 38.8 %copy-start.23 = (bf16[2,16,1,4,128]{4,3,1,0,2:T(4,128)(2,1)}, bf16[2,16,1,4,128]{4,3,1,0,2:T(4,128)(2,1)S(1)}, u32[]{:S(2)}) copy-start(bf16[2,16,1,4,128]{4,3,1,0,2:T(4,128)(2,1)S(1)} %get-tuple-element.129) | copy-start | bytes 98308
  343.5 38.8 %copy-start.25 = (bf16[2,16,1,4,128]{4,3,1,0,2:T(4,128)(2,1)}, bf16[2,16,1,4,128]{4,3,1,0,2:T(4,128)(2,1)S(1)}, u32[]{:S(2)}) copy-start(bf16[2,16,1,4,128]{4,3,1,0,2:T(4,128)(2,1)S(1)} %get-tuple-element.130) | copy-start | bytes 98308
  344.3 38.0 %copy-start.34 = (f32[2,4,16]{2,1,0:T(4,128)}, f32[2,4,16]{2,1,0:T(4,128)S(1)}, u32[]{:S(2)}) copy-start(f32[2,4,16]{2,1,0:T(4,128)S(1)} %get-tuple-element.144) | copy-start | bytes 1540
  348.3 83.8 %all-reduce.15.cloned.1.call-start = ((), (), s32[]{:S(2)}) async-start(), calls=%async_computation.5 | async-start | bytes 393216 | tf_op jit(solution)/shard_map/psum | solution.py:174
  382.3 6.6 collective-permute-start.2
  399.0 87.9 %all-reduce.17.cloned.1.call-start = ((), (), s32[]{:S(2)}) async-start(), calls=%async_computation.6 | async-start | bytes 393216 | tf_op jit(solution)/shard_map/psum | solution.py:190
  433.0 6.6 collective-permute-start.3
  453.9 84.9 %all-reduce.19.cloned.1.call-start = ((), (), s32[]{:S(2)}) async-start(), calls=%async_computation.7 | async-start | bytes 393216 | tf_op jit(solution)/shard_map/psum | solution.py:190
  489.2 7.6 collective-permute-start.4
  500.3 42.1 %copy-start.6 = (bf16[1,32,1,512]{3,1,2,0:T(8,128)(2,1)S(1)}, bf16[1,32,1,512]{3,1,2,0:T(8,128)(2,1)}, u32[]{:S(2)}) copy-start(bf16[1,32,1,512]{3,1,2,0:T(8,128)(2,1)} %stack.162) | copy-start | bytes 98308
  500.3 42.1 %copy-start.7 = (bf16[1,32,1,512]{3,1,2,0:T(8,128)(2,1)S(1)}, bf16[1,32,1,512]{3,1,2,0:T(8,128)(2,1)}, u32[]{:S(2)}) copy-start(bf16[1,32,1,512]{3,1,2,0:T(8,128)(2,1)} %stack.163) | copy-start | bytes 98308
  500.3 42.1 %copy-start.8 = (bf16[1,32,1,512]{3,1,2,0:T(8,128)(2,1)S(1)}, bf16[1,32,1,512]{3,1,2,0:T(8,128)(2,1)}, u32[]{:S(2)}) copy-start(bf16[1,32,1,512]{3,1,2,0:T(8,128)(2,1)} %stack.164) | copy-start | bytes 98308
  500.4 50.9 %copy-start.14 = (bf16[2,16,1,4,128]{4,3,1,0,2:T(4,128)(2,1)S(1)}, bf16[2,16,1,4,128]{4,3,1,0,2:T(4,128)(2,1)}, u32[]{:S(2)}) copy-start(bf16[2,16,1,4,128]{4,3,1,0,2:T(4,128)(2,1)} %copy-done.13) | copy-start | bytes 98308
  500.4 51.0 %copy-start.24 = (bf16[2,16,1,4,128]{4,3,1,0,2:T(4,128)(2,1)S(1)}, bf16[2,16,1,4,128]{4,3,1,0,2:T(4,128)(2,1)}, u32[]{:S(2)}) copy-start(bf16[2,16,1,4,128]{4,3,1,0,2:T(4,128)(2,1)} %copy-done.23) | copy-start | bytes 98308
  500.4 51.0 %copy-start.29 = (f32[2,4,16,16]{2,3,1,0:T(8,128)S(1)}, f32[2,4,16,16]{2,3,1,0:T(8,128)}, u32[]{:S(2)}) copy-start(f32[2,4,16,16]{2,3,1,0:T(8,128)} %get-tuple-element.145) | copy-start | bytes 24580
  500.4 51.0 %copy-start.35 = (f32[2,4,16]{2,1,0:T(4,128)S(1)}, f32[2,4,16]{2,1,0:T(4,128)}, u32[]{:S(2)}) copy-start(f32[2,4,16]{2,1,0:T(4,128)} %copy-done.34) | copy-start | bytes 1540
  507.6 44.0 %copy-start.26 = (bf16[2,16,1,4,128]{4,3,1,0,2:T(4,128)(2,1)S(1)}, bf16[2,16,1,4,128]{4,3,1,0,2:T(4,128)(2,1)}, u32[]{:S(2)}) copy-start(bf16[2,16,1,4,128]{4,3,1,0,2:T(4,128)(2,1)} %copy-done.25) | copy-start | bytes 98308
  507.7 82.9 %all-reduce.21.cloned.1.call-start = ((), (), s32[]{:S(2)}) async-start(), calls=%async_computation.8 | async-start | bytes 393216 | tf_op jit(solution)/shard_map/psum | solution.py:190
  541.1 7.6 collective-permute-start.5
  552.2 7.3 copy-start.5
  559.4 43.6 %copy-start.12 = (bf16[2,16,1,4,128]{4,3,1,0,2:T(4,128)(2,1)S(1)}, bf16[2,16,1,4,128]{4,3,1,0,2:T(4,128)(2,1)}, u32[]{:S(2)}) copy-start(bf16[2,16,1,4,128]{4,3,1,0,2:T(4,128)(2,1)} %copy-done.11) | copy-start | bytes 98308
  559.4 43.8 %copy-start.20 = (bf16[2,16,1,4,128]{4,3,1,0,2:T(4,128)(2,1)S(1)}, bf16[2,16,1,4,128]{4,3,1,0,2:T(4,128)(2,1)}, u32[]{:S(2)}) copy-start(bf16[2,16,1,4,128]{4,3,1,0,2:T(4,128)(2,1)} %copy-done.19) | copy-start | bytes 98308
  559.4 43.8 %copy-start.28 = (f32[2,4,16,16]{2,3,1,0:T(8,128)S(1)}, f32[2,4,16,16]{2,3,1,0:T(8,128)}, u32[]{:S(2)}) copy-start(f32[2,4,16,16]{2,3,1,0:T(8,128)} %get-tuple-element.143) | copy-start | bytes 24580
  559.4 43.8 %copy-start.33 = (f32[2,4,16]{2,1,0:T(4,128)S(1)}, f32[2,4,16]{2,1,0:T(4,128)}, u32[]{:S(2)}) copy-start(f32[2,4,16]{2,1,0:T(4,128)} %copy-done.32) | copy-start | bytes 1540
  559.4 44.0 %copy-start.22 = (bf16[2,16,1,4,128]{4,3,1,0,2:T(4,128)(2,1)S(1)}, bf16[2,16,1,4,128]{4,3,1,0,2:T(4,128)(2,1)}, u32[]{:S(2)}) copy-start(bf16[2,16,1,4,128]{4,3,1,0,2:T(4,128)(2,1)} %copy-done.21) | copy-start | bytes 98308
  559.5 83.0 %all-reduce.23.cloned.1.call-start = ((), (), s32[]{:S(2)}) async-start(), calls=%async_computation.9 | async-start | bytes 393216 | tf_op jit(solution)/shard_map/psum | solution.py:190
  592.9 7.6 collective-permute-start.6
  611.3 44.3 %copy-start.10 = (bf16[2,16,1,4,128]{4,3,1,0,2:T(4,128)(2,1)S(1)}, bf16[2,16,1,4,128]{4,3,1,0,2:T(4,128)(2,1)}, u32[]{:S(2)}) copy-start(bf16[2,16,1,4,128]{4,3,1,0,2:T(4,128)(2,1)} %copy-done.9) | copy-start | bytes 98308
  611.3 44.4 %copy-start.16 = (bf16[2,16,1,4,128]{4,3,1,0,2:T(4,128)(2,1)S(1)}, bf16[2,16,1,4,128]{4,3,1,0,2:T(4,128)(2,1)}, u32[]{:S(2)}) copy-start(bf16[2,16,1,4,128]{4,3,1,0,2:T(4,128)(2,1)} %copy-done.15) | copy-start | bytes 98308
  611.3 44.4 %copy-start.31 = (f32[2,4,16]{2,1,0:T(4,128)S(1)}, f32[2,4,16]{2,1,0:T(4,128)}, u32[]{:S(2)}) copy-start(f32[2,4,16]{2,1,0:T(4,128)} %copy-done.30) | copy-start | bytes 1540
  611.3 45.6 %copy-start.18 = (bf16[2,16,1,4,128]{4,3,1,0,2:T(4,128)(2,1)S(1)}, bf16[2,16,1,4,128]{4,3,1,0,2:T(4,128)(2,1)}, u32[]{:S(2)}) copy-start(bf16[2,16,1,4,128]{4,3,1,0,2:T(4,128)(2,1)} %copy-done.17) | copy-start | bytes 98308
  611.3 275.4 %reduce-scatter.2.cloned.1.call-start = ((), (), s32[]{:S(2)}) async-start(), calls=%async_computation.10 | async-start | bytes 15728640 | tf_op jit(solution)/shard_map/reduce_scatter | solution.py:223
  644.8 7.6 collective-permute-start.7
  (6 other events, 19.8 us)
Sparse Core Ops, SparseCore 0:
  12.3 220.9 all-gather.1
  248.7 29.8 all-reduce.8
  297.0 32.8 all-reduce.10
  348.4 32.8 all-reduce.12
  399.1 32.8 all-reduce.14
  454.0 32.8 all-reduce.16
  507.8 30.9 all-reduce.18
  559.6 30.9 all-reduce.20
  611.5 30.9 all-reduce.22
  675.6 211.1 reduce-scatter.1
where the time goes:
time: 911 us; the launch traced here: 910 us
  waiting for transfers between devices  697 us (77%)
  matrix products  100 us (11%)
  other arithmetic  41.1 us (5%)
  starting transfers between devices  19.5 us (2%)
  blocking collectives  17.9 us (2%)
  local copies, waits for them, and re-layouts  16 us (2%)
  between operations  15.4 us (2%)
    reduce_scatter x1, waiting for transfers between devices, shards(): lax.psum_scatter(blocks.reshape(rows_here * lax.axis_size('dp'), blocks.s...  211 us
    all_gather x1, waiting for transfers between devices, shards(): lax.all_gather(master_weights[0].astype(jnp.bfloat16), 'dp', axis=0, tile...  207 us
    psum x4, waiting for transfers between devices, shards(): summed = lax.psum(d_terms.astype(jnp.bfloat16), 'mp').astype(jnp.float32)  124 us
    psum x4, waiting for transfers between devices, shards(): mixed = lax.psum(head_part.astype(jnp.bfloat16), 'mp').astype(jnp.float32)  120 us
    ppermute x8, waiting for transfers between devices, from_behind(): return lax.ppermute(array, axis, pairs)  34 us
    dot_general x4, matrix products, feature_terms(): jnp.einsum('nsc,sdc->nd', d_project, triple, preferred_element_type=jnp.f...  28.8 us
    dot_general x5, matrix products, layer_local(): jnp.einsum('nd,sdc->nsc', normed, triple, preferred_element_type=jnp.floa...  23.5 us
    ppermute x8, starting transfers between devices, from_behind(): return lax.ppermute(array, axis, pairs)  19.1 us
  transfers between devices with their start and end apart: 18, of which 18 were waited for; matrix products, arithmetic and copies ran while one was open for 1% of the time, Pallas kernels for 0%

commit v1 on v0

--- a/solution.py
+++ b/solution.py
@@ -231,6 +231,180 @@
     )
     return (new_master[None], new_first[None], new_second[None])
 
+def block_positions(visible_index, model_width, block_width):
+    half_width = model_width // 2
+    place = lax.axis_index("mp") * block_width + jnp.arange(block_width, dtype=jnp.int32)
+    rate = jnp.exp(
+        (place % half_width).astype(jnp.float32) * (-2.0 * math.log(10000.0) / model_width)
+    )
+    angles = visible_index.astype(jnp.float32)[..., None] * rate
+    return jnp.where(place < half_width, jnp.sin(angles), jnp.cos(angles))
+
+
+def gather_tokens(block):
+    return lax.all_gather(
+        lax.all_gather(block, "dp", axis=0, tiled=True), "mp", axis=1, tiled=True
+    )
+
+
+def exchange_rows(array):
+    return lax.all_to_all(array, "dp", 0, 0, tiled=True)
+
+
+def gather_rows(array):
+    return lax.all_gather(array, "dp", axis=0, tiled=True)
+
+
+def scatter_features(array):
+    return lax.psum_scatter(array, "mp", scatter_dimension=1, tiled=True)
+
+
+def scatter_from_last(array):
+    rows = array.shape[0] // lax.axis_size("dp")
+    return exchange_rows(array)[-rows:]
+
+
+def row_sums(array):
+    return jnp.sum(lax.all_gather(array, "mp", axis=0), axis=0)
+
+
+def sum_rows(array):
+    peers = lax.axis_size("dp")
+    parts = exchange_rows(array).reshape(peers, array.shape[0] // peers, array.shape[1])
+    return jnp.sum(parts[: peers - 1].astype(jnp.float32), axis=0)
+
+
+def split_heads(array, length):
+    return array.reshape(-1, length, array.shape[-1] // HD, HD)
+
+
+def attend(queries, key_rows, values, length):
+    queries, key_rows, values = (split_heads(part, length) for part in (queries, key_rows, values))
+    scores = jnp.einsum(
+        "vqhe,vkhe->vhqk", queries, key_rows, preferred_element_type=jnp.float32
+    ) * (1.0 / math.sqrt(HD))
+    probs = softmax_rows(scores)
+    attended = jnp.einsum(
+        "vhqk,vkhe->vqhe",
+        probs.astype(jnp.bfloat16),
+        values,
+        preferred_element_type=jnp.float32,
+    )
+    return (probs, attended.astype(jnp.bfloat16).reshape(-1, attended.shape[2] * HD))
+
+
+def attend_back(queries, key_rows, values, probs, d_attended, length):
+    queries, key_rows, values, d_attended = (
+        split_heads(part, length) for part in (queries, key_rows, values, d_attended)
+    )
+    d_probs = jnp.einsum(
+        "vqhe,vkhe->vhqk", d_attended, values, preferred_element_type=jnp.float32
+    )
+    d_scores = (
+        probs
+        * (d_probs - jnp.sum(d_probs * probs, axis=-1, keepdims=True))
+        * (1.0 / math.sqrt(HD))
+    ).astype(jnp.bfloat16)
+    d_queries = jnp.einsum(
+        "vhqk,vkhe->vqhe", d_scores, key_rows, preferred_element_type=jnp.float32
+    )
+    d_keys = jnp.einsum("vhqk,vqhe->vkhe", d_scores, queries, preferred_element_type=jnp.float32)
+    d_values = jnp.einsum(
+        "vhqk,vqhe->vkhe",
+        probs.astype(jnp.bfloat16),
+        d_attended,
+        preferred_element_type=jnp.float32,
+    )
+    return tuple(
+        part.astype(jnp.bfloat16).reshape(-1, part.shape[2] * HD)
+        for part in (d_queries, d_keys, d_values)
+    )
+
+
+def times_weights(left, weights):
+    return jnp.dot(left, weights, preferred_element_type=jnp.float32).astype(jnp.bfloat16)
+
+
+def times_weights_t(left, weights):
+    return lax.dot_general(
+        left, weights, (((1,), (1,)), ((), ())), preferred_element_type=jnp.float32
+    ).astype(jnp.bfloat16)
+
+
+def still_shards(
+    patch_tokens, visible_index, output_grad, norm_gain, master_weights, first_moment, second_moment
+):
+    peers = lax.axis_size("dp")
+    vol_count, length, block_width = patch_tokens.shape
+    model_width = block_width * lax.axis_size("mp")
+    rows = vol_count * length
+    in_first = lax.axis_index("segment") == 0
+    holds_out = lax.axis_index("dp") == peers - 1
+    norm_scale = norm_gain[0]
+    weights = master_weights[0].astype(jnp.bfloat16)
+    own_input = (
+        patch_tokens.astype(jnp.float32) + block_positions(visible_index, model_width, block_width)
+    ).astype(jnp.bfloat16)
+    own_input = own_input.reshape(rows, block_width)
+    own_grad = output_grad.reshape(rows, block_width)
+
+    def parts_of(array):
+        return [array[i * rows : (i + 1) * rows] for i in range(peers)]
+
+    entered = gather_tokens(jnp.where(in_first, own_input, own_grad))
+    normed = norm_forward(entered, norm_scale)[0]
+    left_first = jnp.where(holds_out, entered, normed)
+    q0, k0, v0, _ = parts_of(exchange_rows(times_weights(left_first, weights)))
+    probs0, attended0 = attend(q0, k0, v0, length)
+    mixed = scatter_from_last(
+        scatter_features(times_weights_t(gather_rows(attended0), weights))
+    )
+    own_out = (own_input.astype(jnp.float32) + mixed.astype(jnp.float32)).astype(jnp.bfloat16)
+    own_out = lax.ppermute(own_out, "segment", [(0, 1)])
+
+    middle = gather_tokens(own_out)
+    left_second = jnp.where(holds_out, entered, norm_forward(middle, norm_scale)[0])
+    q1, k1, v1, da1 = parts_of(exchange_rows(times_weights(left_second, weights)))
+    probs1, attended1 = attend(q1, k1, v1, length)
+    grads1 = attend_back(q1, k1, v1, probs1, da1, length)
+    right_second = exchange_rows(jnp.concatenate(grads1 + (attended1,), axis=0))
+    d_normed = sum_rows(scatter_features(times_weights_t(right_second, weights)))
+
+    own_rows = lax.dynamic_slice_in_dim(middle, lax.axis_index("dp") * rows, rows, 0)
+    own_cols = lax.axis_index("mp") * block_width
+    _, standard, inverse_dev = norm_forward(own_rows, norm_scale)
+    standard = lax.dynamic_slice_in_dim(standard, own_cols, block_width, 1)
+    scaled = d_normed * lax.dynamic_slice_in_dim(norm_scale, own_cols, block_width, 0)
+    sums = row_sums(
+        jnp.stack([jnp.sum(scaled, axis=-1), jnp.sum(scaled * standard, axis=-1)])
+    ) * (1.0 / model_width)
+    inner = scaled - sums[0][:, None] - standard * sums[1][:, None]
+    own_d = (own_grad.astype(jnp.float32) + inner * inverse_dev).astype(jnp.bfloat16)
+    own_d = lax.ppermute(own_d, "segment", [(1, 0)])
+
+    returned = gather_tokens(own_d)
+    da0 = scatter_from_last(times_weights(returned, weights))
+    grads0 = attend_back(q0, k0, v0, probs0, da0, length)
+    right_first = exchange_rows(jnp.concatenate(grads0 + (attended0,), axis=0))
+
+    left_first = jnp.where(holds_out, returned, normed)
+    left_side = jnp.where(in_first, left_first, left_second)
+    right_side = jnp.where(in_first, right_first, right_second)
+    gradient = lax.dot_general(
+        left_side, right_side, (((0,), (0,)), ((), ())), preferred_element_type=jnp.float32
+    )
+    new_master, new_first, new_second = adam_update(
+        gradient, master_weights[0], first_moment[0], second_moment[0]
+    )
+    return (new_master[None], new_first[None], new_second[None])
+
+
+def section_step(*arrays):
+    model_width = arrays[0].shape[2] * lax.axis_size("mp")
+    if arrays[4].shape[1] == model_width and lax.axis_size("dp") == 4:
+        return still_shards(*arrays)
+    return shards(*arrays)
+
 
 def solution(mesh):
     placed = (
@@ -243,7 +417,7 @@
         P("segment", "dp", "mp"),
     )
     return jax.shard_map(
-        shards,
+        section_step,
         mesh=mesh,
         in_specs=placed,
         out_specs=(P("segment", "dp", "mp"), P("segment", "dp", "mp"), P("segment", "dp", "mp")),

time: 911 us -> 500 us (0.55)
  waiting for transfers between devices: 697 us -> 181 us
  blocking collectives: 17.9 us -> 196 us
  matrix products: 100 us -> 58.6 us
  other arithmetic: 41.1 us -> 25 us
  starting transfers between devices: 19.5 us -> 9.45 us
    psum x8 -> x0, waiting for transfers between devices: 244 us -> none  [the longest x4 124 us: shards(): summed = lax.psum(d_terms.astype(jnp.bfloat16), 'mp').astype(jnp.float32)]
    reduce_scatter x1 -> x2, waiting for transfers between devices: 211 us -> 72.3 us  [scatter_features(): return lax.psum_scatter(array, 'mp', scatter_dimension=1, tiled=True)]
    all_gather x1 -> x3, waiting for transfers between devices: 207 us -> 79.9 us  [gather_tokens(): lax.all_gather(lax.all_gather(block, 'dp', axis=0, tiled=True), 'mp', axi...]
    all_to_all x0 -> x6, blocking collectives: none -> 117 us  [exchange_rows(): return lax.all_to_all(array, 'dp', 0, 0, tiled=True)]
    all_gather x2 -> x5, blocking collectives: 17.9 us -> 79 us  [the longest x3 58.2 us: gather_tokens(): lax.all_gather(block, 'dp', axis=0, tiled=True)]
    dot_general x47 -> x16, matrix products: 97.5 us -> 54.1 us  [the longest x1 16.8 us: still_shards(): lax.dot_general(left_side, right_side, (((0,), (0,)), ((), ())), preferre...]
    ppermute x8 -> x2, waiting for transfers between devices: 34 us -> 10.9 us  [the longest x1 7.72 us: still_shards(): own_d = lax.ppermute(own_d, 'segment', [(1, 0)])]
    all_to_all x0 -> x1, waiting for transfers between devices: none -> 17.9 us  [exchange_rows(): return lax.all_to_all(array, 'dp', 0, 0, tiled=True)]
  transfers between devices with their start and end apart: 18 -> 8, of which waited for: 18 -> 8; matrix products, arithmetic and copies ran while one was open for 1% -> 1% of each run, Pallas kernels for 0% -> 0%
where the time goes in v1:
time: 500 us; the launch traced here: 499 us
  blocking collectives  196 us (39%)
  waiting for transfers between devices  181 us (36%)
  matrix products  58.6 us (12%)
  other arithmetic  25 us (5%)
  local copies, waits for them, and re-layouts  15 us (3%)
  between operations  14.2 us (3%)
  starting transfers between devices  9.45 us (2%)
    all_to_all x6, blocking collectives, exchange_rows(): return lax.all_to_all(array, 'dp', 0, 0, tiled=True)  117 us
    all_gather x3, waiting for transfers between devices, gather_tokens(): lax.all_gather(lax.all_gather(block, 'dp', axis=0, tiled=True), 'mp', axi...  79.9 us
    reduce_scatter x2, waiting for transfers between devices, scatter_features(): return lax.psum_scatter(array, 'mp', scatter_dimension=1, tiled=True)  72.3 us
    all_gather x3, blocking collectives, gather_tokens(): lax.all_gather(block, 'dp', axis=0, tiled=True)  58.2 us
    all_to_all x1, waiting for transfers between devices, exchange_rows(): return lax.all_to_all(array, 'dp', 0, 0, tiled=True)  17.9 us
    dot_general x1, matrix products, still_shards(): lax.dot_general(left_side, right_side, (((0,), (0,)), ((), ())), preferre...  16.8 us
    all_gather x1, blocking collectives, gather_rows(): return lax.all_gather(array, 'dp', axis=0, tiled=True)  15.7 us
    dot_general x3, matrix products, times_weights(): jnp.dot(left, weights, preferred_element_type=jnp.float32)  10.3 us
  transfers between devices with their start and end apart: 8, of which 8 were waited for; matrix products, arithmetic and copies ran while one was open for 1% of the time, Pallas kernels for 0%

profile of v1, /device:TPU:0, one launch (start us, length us, event | category | flops | bytes accessed | tf_op | source)
XLA Modules:
  0.0 499.1 jit_solution(6843259343717020021)
XLA Ops:
  7.9 2.5 broadcast_select_fusion
  10.5 21.7 %all_gather.27 = bf16[512,768]{1,0:T(8,128)(2,1)} all-gather(bf16[128,768]{1,0:T(8,128)(2,1)S(1)} %bitcast.132), channel_id=1, replica_groups=mesh['segment'=2,'dp'=4,'mp'=4] {'dp'}, dimensions={0}, use_global_device_ids=true | all-gather | bytes 983040 | tf_op jit(solution)/shard_map/all_gather | solution.py:246
  32.3 3.2 bitcast_convert_fusion
  35.5 25.1 %all-gather.6.cloned.1.call-done = bf16[512,3072]{1,0:T(8,128)(2,1)} async-done(((bf16[512,768]{1,0:T(8,128)(2,1)}), bf16[512,3072]{1,0:T(8,128)(2,1)}) %all-gather.6.cloned.1.call-update) | async-done | bytes 3145744 | tf_op jit(solution)/shard_map/all_gather | solution.py:245
  60.6 2.5 convert_reduce_fusion.1
  63.2 2.8 fusion.11
  66.1 1.9 fusion.39
  68.0 19.3 %all_to_all.69 = bf16[4,128,512]{2,1,0:T(8,128)(2,1)S(1)} all-to-all(bf16[4,128,512]{2,1,0:T(8,128)(2,1)S(1)} %bitcast.134), channel_id=1, replica_groups=mesh['segment'=2,'dp'=4,'mp'=4] {'dp'}, dimensions={0} | all-to-all | bytes 1048576 | tf_op jit(solution)/shard_map/all_to_all | solution.py:251
  88.0 1.6 reshape.171
  91.2 2.0 fusion.174
  93.2 2.1 fusion.54
  96.9 15.7 %all_gather.29 = bf16[512,512]{1,0:T(8,128)(2,1)S(1)} all-gather(bf16[128,512]{1,0:T(8,128)(2,1)S(1)} %bitcast.128), channel_id=1, replica_groups=mesh['segment'=2,'dp'=4,'mp'=4] {'dp'}, dimensions={0}, use_global_device_ids=true | all-gather | bytes 655360 | tf_op jit(solution)/shard_map/all_gather | solution.py:255
  112.6 3.6 convolution_convert_fusion.1
  116.3 36.1 %reduce-scatter.3.cloned.1.call-done = bf16[512,768]{1,0:T(8,128)(2,1)} async-done(((bf16[512,3072]{1,0:T(8,128)(2,1)}), bf16[512,768]{1,0:T(8,128)(2,1)}) %reduce-scatter.3.cloned.1.call-update) | async-done | bytes 786448 | tf_op jit(solution)/shard_map/reduce_scatter | solution.py:259
  152.3 24.7 %all_to_all.70 = bf16[4,128,768]{2,1,0:T(8,128)(2,1)S(1)} all-to-all(bf16[4,128,768]{2,1,0:T(8,128)(2,1)} %bitcast.131), channel_id=1, replica_groups=mesh['segment'=2,'dp'=4,'mp'=4] {'dp'}, dimensions={0} | all-to-all | bytes 1572864 | tf_op jit(solution)/shard_map/all_to_all | solution.py:251
  177.1 3.4 collective-permute-start
  180.5 3.2 collective-permute-done
  183.7 18.1 %all_gather.30 = bf16[512,768]{1,0:T(8,128)(2,1)} all-gather(bf16[128,768]{1,0:T(8,128)(2,1)S(1)} %collective-permute-done), channel_id=1, replica_groups=mesh['segment'=2,'dp'=4,'mp'=4] {'dp'}, dimensions={0}, use_global_device_ids=true | all-gather | bytes 983040 | tf_op jit(solution)/shard_map/all_gather | solution.py:246
  201.9 28.8 %all-gather.8.cloned.1.call-done = bf16[512,3072]{1,0:T(8,128)(2,1)} async-done(((bf16[512,768]{1,0:T(8,128)(2,1)}), bf16[512,3072]{1,0:T(8,128)(2,1)}) %all-gather.8.cloned.1.call-update) | async-done | bytes 3145744 | tf_op jit(solution)/shard_map/all_gather | solution.py:245
  230.7 2.5 convert_reduce_fusion
  233.2 2.8 fusion.8
  236.1 3.7 convolution_convert_fusion.3
  239.9 20.3 %all_to_all.71 = bf16[4,128,512]{2,1,0:T(8,128)(2,1)S(1)} all-to-all(bf16[4,128,512]{2,1,0:T(8,128)(2,1)S(1)} %bitcast.135), channel_id=1, replica_groups=mesh['segment'=2,'dp'=4,'mp'=4] {'dp'}, dimensions={0} | all-to-all | bytes 1048576 | tf_op jit(solution)/shard_map/all_to_all | solution.py:251
  261.8 1.6 reshape.175
  265.0 2.5 fusion.179
  267.5 2.0 fusion.59
  269.5 1.4 fusion.56
  270.9 1.6 fusion.58
  272.6 2.3 fusion.55
  277.0 16.6 %all_to_all.72 = bf16[4,128,512]{2,1,0:T(8,128)(2,1)S(1)} all-to-all(bf16[4,128,512]{2,1,0:T(8,128)(2,1)S(1)} %bitcast.126), channel_id=1, replica_groups=mesh['segment'=2,'dp'=4,'mp'=4] {'dp'}, dimensions={0} | all-to-all | bytes 1048576 | tf_op jit(solution)/shard_map/all_to_all | solution.py:251
  294.4 6.3 %convolution_convert_fusion = bf16[512,3072]{1,0:T(8,128)(2,1)} fusion(bf16[512,512]{1,0:T(8,128)(2,1)S(1)} %bitcast.125, f32[1,3072,512]{2,1,0:T(8,128)} %param.11), kind=kOutput, calls=%fused_computation.27 | convolution fusion | flops 1613758464 | bytes 9961472 | tf_op jit(solution)/shard_map/dot_general | solution.py:329
  300.7 36.2 %reduce-scatter.5.cloned.1.call-done = bf16[512,768]{1,0:T(8,128)(2,1)} async-done(((bf16[512,3072]{1,0:T(8,128)(2,1)}), bf16[512,768]{1,0:T(8,128)(2,1)}) %reduce-scatter.5.cloned.1.call-update) | async-done | bytes 786448 | tf_op jit(solution)/shard_map/reduce_scatter | solution.py:259
  336.9 4.6 all-to-all-start.4
  342.5 1.4 multiply_reduce_fusion
  343.9 17.9 %all-to-all-done.4 = bf16[4,128,768]{2,1,0:T(8,128)(2,1)} async-done(((bf16[4,128,768]{2,1,0:T(8,128)(2,1)}), bf16[4,128,768]{2,1,0:T(8,128)(2,1)}, u32[]{:S(2)}, u32[]{:S(2)}) %all-to-all-start.4) | async-done | bytes 786464 | tf_op jit(solution)/shard_map/all_to_all | solution.py:251
  364.1 5.1 %all-gather.1 = f32[4,2,128]{2,1,0:T(2,128)S(1)} all-gather(f32[1,2,128]{2,1,0:T(2,128)S(1)} %maximum_bitcast_fusion), channel_id=2, replica_groups=mesh['segment'=2,'dp'=4,'mp'=4] {'mp'}, dimensions={0}, use_global_device_ids=true | all-gather | bytes 5120 | tf_op jit(solution)/shard_map/all_gather | solution.py:268
  371.7 1.3 collective-permute-start.1
  373.0 7.7 %collective-permute-done.1 = bf16[128,768]{1,0:T(8,128)(2,1)S(1)} collective-permute-done((bf16[128,768]{1,0:T(8,128)(2,1)S(1)}, bf16[128,768]{1,0:T(8,128)(2,1)S(1)}, u32[]{:S(2)}, u32[]{:S(2)}) %collective-permute-start.1) | collective-permute-done | bytes 196640 | tf_op jit(solution)/shard_map/ppermute | solution.py:383
  380.7 18.3 %all_gather.34 = bf16[512,768]{1,0:T(8,128)(2,1)} all-gather(bf16[128,768]{1,0:T(8,128)(2,1)S(1)} %collective-permute-done.1), channel_id=1, replica_groups=mesh['segment'=2,'dp'=4,'mp'=4] {'dp'}, dimensions={0}, use_global_device_ids=true | all-gather | bytes 983040 | tf_op jit(solution)/shard_map/all_gather | solution.py:246
  399.1 25.9 %all-gather.10.cloned.1.call-done = bf16[512,3072]{1,0:T(8,128)(2,1)} async-done(((bf16[512,768]{1,0:T(8,128)(2,1)}), bf16[512,3072]{1,0:T(8,128)(2,1)}) %all-gather.10.cloned.1.call-update) | async-done | bytes 3145744 | tf_op jit(solution)/shard_map/all_gather | solution.py:245
  425.0 4.6 convolution_convert_fusion.2
  429.7 19.4 %all_to_all.73 = bf16[4,128,512]{2,1,0:T(8,128)(2,1)S(1)} all-to-all(bf16[4,128,512]{2,1,0:T(8,128)(2,1)S(1)} %bitcast.133), channel_id=1, replica_groups=mesh['segment'=2,'dp'=4,'mp'=4] {'dp'}, dimensions={0} | all-to-all | bytes 1048576 | tf_op jit(solution)/shard_map/all_to_all | solution.py:251
  449.8 1.8 fusion.80
  451.7 1.4 fusion.61
  453.1 1.5 fusion.57
  454.6 2.2 fusion.60
  458.0 16.6 %all_to_all.74 = bf16[4,128,512]{2,1,0:T(8,128)(2,1)S(1)} all-to-all(bf16[4,128,512]{2,1,0:T(8,128)(2,1)S(1)} %bitcast.127), channel_id=1, replica_groups=mesh['segment'=2,'dp'=4,'mp'=4] {'dp'}, dimensions={0} | all-to-all | bytes 1048576 | tf_op jit(solution)/shard_map/all_to_all | solution.py:251
  475.8 16.8 %fusion.38 = (f32[1,3072,512]{2,1,0:T(8,128)}, f32[1,3072,512]{2,1,0:T(8,128)}, f32[1,3072,512]{2,1,0:T(8,128)}) fusion(f32[1,3072,512]{2,1,0:T(8,128)} %param.13, f32[1,3072,512]{2,1,0:T(8,128)} %param.12, f32[1,3072,512]{2,1,0:T(8,128)} %param.11, bf16[512,512]{1,0:T(8,128)(2,1)S(1)} %bitcast_select_fusion, ...), kind=kOutput, calls=%fused_computation.49 | convolution fusion | flops 1654652928 | bytes 47730688 | tf_op jit(solution)/shard_map/dot_general | solution.py:393
  (88 shorter events, 20.0 us)
Async XLA Ops:
  7.2 53.5 %all-gather.6.cloned.1.call-start = ((), (), s32[]{:S(2)}) async-start(), calls=%async_computation.9 | async-start | bytes 3932160 | tf_op jit(solution)/shard_map/all_gather | solution.py:245
  32.2 120.1 %reduce-scatter.3.cloned.1.call-start = ((), (), s32[]{:S(2)}) async-start(), calls=%async_computation.10 | async-start | bytes 3932160 | tf_op jit(solution)/shard_map/reduce_scatter | solution.py:259
  32.3 33.8 %copy-start.14 = (f32[1,3072]{1,0:T(1,128)S(1)}, f32[1,3072]{1,0:T(1,128)}, u32[]{:S(2)}) copy-start(f32[1,3072]{1,0:T(1,128)} %param.10) | copy-start | bytes 36868
  35.5 77.1 %copy-start.2 = (bf16[3072,512]{1,0:T(8,128)(2,1)}, bf16[3072,512]{1,0:T(8,128)(2,1)S(1)}, u32[]{:S(2)}) copy-start(bf16[3072,512]{1,0:T(8,128)(2,1)S(1)} %bitcast_convert_fusion) | copy-start | bytes 9437188
  60.6 5.4 %copy-start.1 = (bf16[512,3072]{1,0:T(8,128)(2,1)S(1)}, bf16[512,3072]{1,0:T(8,128)(2,1)}, u32[]{:S(2)}) copy-start(bf16[512,3072]{1,0:T(8,128)(2,1)} %all-gather.6.cloned.1.call-done) | copy-start | bytes 9437188
  66.0 1.9 copy-start.10
  91.2 25.0 %copy-start.6 = (bf16[8,16,4,128]{3,2,1,0:T(4,128)(2,1)}, bf16[8,16,4,128]{3,2,1,0:T(4,128)(2,1)S(1)}, u32[]{:S(2)}) copy-start(bf16[8,16,4,128]{3,2,1,0:T(4,128)(2,1)S(1)} %reshape.170) | copy-start | bytes 393220
  93.2 23.0 %copy-start.15 = (f32[8,4,16]{2,1,0:T(4,128)}, f32[8,4,16]{2,1,0:T(4,128)S(1)}, u32[]{:S(2)}) copy-start(f32[8,4,16]{2,1,0:T(4,128)S(1)} %get-tuple-element.21) | copy-start | bytes 6148
  96.3 0.6 copy-start.4
  116.2 114.5 %all-gather.8.cloned.1.call-start = ((), (), s32[]{:S(2)}) async-start(), calls=%async_computation.11 | async-start | bytes 3932160 | tf_op jit(solution)/shard_map/all_gather | solution.py:245
  177.1 6.6 %collective-permute-start = (bf16[128,768]{1,0:T(8,128)(2,1)S(1)}, bf16[128,768]{1,0:T(8,128)(2,1)S(1)}, u32[]{:S(2)}, u32[]{:S(2)}) collective-permute-start(bf16[128,768]{1,0:T(8,128)(2,1)S(1)} %fusion.73), channel_id=1, source_target_pairs={{0,16},{1,17},{2,18},{3,19},{4,20},{5,21},{6,22},{7,23},{8,24},{9,... | collective-permute-start | bytes 589832 | tf_op jit(solution)/shard_map/ppermute | solution.py:363
  201.9 135.1 %reduce-scatter.5.cloned.1.call-start = ((), (), s32[]{:S(2)}) async-start(), calls=%async_computation.12 | async-start | bytes 3932160 | tf_op jit(solution)/shard_map/reduce_scatter | solution.py:259
  230.7 5.4 %copy-start = (bf16[512,3072]{1,0:T(8,128)(2,1)S(1)}, bf16[512,3072]{1,0:T(8,128)(2,1)}, u32[]{:S(2)}) copy-start(bf16[512,3072]{1,0:T(8,128)(2,1)} %all-gather.8.cloned.1.call-done) | copy-start | bytes 9437188
  236.1 3.8 copy-start.12
  264.1 8.4 %copy-start.8 = (bf16[8,16,4,128]{3,2,1,0:T(4,128)(2,1)S(1)}, bf16[8,16,4,128]{3,2,1,0:T(4,128)(2,1)}, u32[]{:S(2)}) copy-start(bf16[8,16,4,128]{3,2,1,0:T(4,128)(2,1)} %reshape.174) | copy-start | bytes 393220
  293.6 0.8 copy-start.3
  336.9 24.8 %all-to-all-start.4 = ((bf16[4,128,768]{2,1,0:T(8,128)(2,1)}), bf16[4,128,768]{2,1,0:T(8,128)(2,1)}, u32[]{:S(2)}, u32[]{:S(2)}) async-start(bf16[4,128,768]{2,1,0:T(8,128)(2,1)} %bitcast.130), calls=%async_computation.6 | async-start | bytes 1572864 | tf_op jit(solution)/shard_map/all_to_all | solution.py:251
  341.5 83.5 %all-gather.10.cloned.1.call-start = ((), (), s32[]{:S(2)}) async-start(), calls=%async_computation.13 | async-start | bytes 3932160 | tf_op jit(solution)/shard_map/all_gather | solution.py:245
  343.9 20.3 %copy-start.9 = (f32[128]{0:T(128)}, f32[128]{0:T(128)S(1)}, u32[]{:S(2)}) copy-start(f32[128]{0:T(128)S(1)} %add_rsqrt_fusion.2) | copy-start | bytes 1540
  371.7 9.0 %collective-permute-start.1 = (bf16[128,768]{1,0:T(8,128)(2,1)S(1)}, bf16[128,768]{1,0:T(8,128)(2,1)S(1)}, u32[]{:S(2)}, u32[]{:S(2)}) collective-permute-start(bf16[128,768]{1,0:T(8,128)(2,1)S(1)} %fusion.74), channel_id=1, source_target_pairs={{16,0},{17,1},{18,2},{19,3},{20,4},{21,5},{22,6},{23,7},{24,8},{25... | collective-permute-start | bytes 589832 | tf_op jit(solution)/shard_map/ppermute | solution.py:383
  399.1 50.7 %copy-start.7 = (bf16[8,16,4,128]{3,2,1,0:T(4,128)(2,1)S(1)}, bf16[8,16,4,128]{3,2,1,0:T(4,128)(2,1)}, u32[]{:S(2)}) copy-start(bf16[8,16,4,128]{3,2,1,0:T(4,128)(2,1)} %copy-done.6) | copy-start | bytes 393220
  429.7 28.3 %copy-start.5 = (bf16[16,8,4,128]{3,1,2,0:T(8,128)(2,1)S(1)}, bf16[16,8,4,128]{3,1,2,0:T(8,128)(2,1)}, u32[]{:S(2)}) copy-start(bf16[16,8,4,128]{3,1,2,0:T(8,128)(2,1)} %copy-done.4) | copy-start | bytes 393220
  429.7 46.1 %copy-start.11 = (f32[512]{0:T(512)S(1)}, f32[512]{0:T(512)}, u32[]{:S(2)}) copy-start(f32[512]{0:T(512)} %copy-done.10) | copy-start | bytes 6148
  429.7 46.1 %copy-start.13 = (f32[512]{0:T(512)S(1)}, f32[512]{0:T(512)}, u32[]{:S(2)}) copy-start(f32[512]{0:T(512)} %copy-done.12) | copy-start | bytes 6148
Sparse Core Ops, SparseCore 0:
  32.3 28.2 all-gather.5
  116.3 35.9 reduce-scatter.2
  202.0 28.6 all-gather.7
  300.8 36.0 reduce-scatter.4
  399.2 25.7 all-gather.9

commit v2 on v1

--- a/solution.py
+++ b/solution.py
@@ -1,8 +1,11 @@
+import functools
 import math
 
 import jax
 import jax.numpy as jnp
 from jax import lax
+from jax.experimental import pallas as pl
+from jax.experimental.pallas import tpu as pltpu
 from jax.sharding import PartitionSpec as P
 
 HD = 128
@@ -241,22 +244,245 @@
     return jnp.where(place < half_width, jnp.sin(angles), jnp.cos(angles))
 
 
+def greet(partners):
+    barrier = pltpu.get_barrier_semaphore()
+    for partner in partners:
+        pl.semaphore_signal(
+            barrier, inc=1, device_id=partner, device_id_type=pl.DeviceIdType.MESH
+        )
+    pl.semaphore_wait(barrier, len(partners))
+
+
+def push(source, target, send_sem, recv_sem, partner):
+    return pltpu.make_async_remote_copy(
+        src_ref=source,
+        dst_ref=target,
+        send_sem=send_sem,
+        recv_sem=recv_sem,
+        device_id=partner,
+        device_id_type=pl.DeviceIdType.MESH,
+    )
+
+
+def in_vmem(kernel, operand, out_shape, scratch, collective_id):
+    return pl.pallas_call(
+        kernel,
+        out_shape=out_shape,
+        in_specs=[pl.BlockSpec(memory_space=pltpu.VMEM)],
+        out_specs=pl.BlockSpec(memory_space=pltpu.VMEM),
+        scratch_shapes=scratch,
+        compiler_params=pltpu.CompilerParams(
+            collective_id=collective_id, has_side_effects=True, vmem_limit_bytes=40 * 2**20
+        ),
+    )(operand)
+
+
+def mesh_partners(peers):
+    row, col = lax.axis_index("dp"), lax.axis_index("mp")
+    along = [{"dp": lax.rem(row + step, peers)} for step in range(1, peers)]
+    across = {"mp": lax.rem(col + 2, 4)}
+    beside = {"mp": col + 1 - 2 * lax.rem(col, 2)}
+    return (along, across, beside)
+
+
+def gather_kernel(peers, x_ref, o_ref, z_send, z_recv, y_send, y_recv, c_send, c_recv):
+    rows, width = x_ref.shape
+    row, col = lax.axis_index("dp"), lax.axis_index("mp")
+    along, across, beside = mesh_partners(peers)
+    greet(along + [across, beside])
+
+    def place(step, owner):
+        source = lax.rem(row - step + peers, peers)
+        return o_ref.at[
+            pl.ds(pl.multiple_of(source * rows, rows), rows),
+            pl.ds(pl.multiple_of(owner * width, width), width),
+        ]
+
+    over = lax.rem(col + 2, 4)
+    along_copies = [
+        push(x_ref, place(0, col), z_send.at[step], z_recv.at[step], along[step])
+        for step in range(peers - 1)
+    ]
+    for copy in along_copies:
+        copy.start()
+    across_copies, beside_copies = [], []
+    for step in range(peers):
+        source = x_ref
+        if step > 0:
+            along_copies[step - 1].wait_recv()
+            source = place(step, col)
+        across_copies.append(
+            push(source, place(step, col), y_send.at[step], y_recv.at[step], across)
+        )
+        across_copies[-1].start()
+        beside_copies.append(
+            push(source, place(step, col), c_send.at[step], c_recv.at[step], beside)
+        )
+        beside_copies[-1].start()
+    own_rows = pl.ds(pl.multiple_of(row * rows, rows), rows)
+    o_ref[own_rows, pl.ds(pl.multiple_of(col * width, width), width)] = x_ref[...]
+    for step in range(peers):
+        across_copies[step].wait_recv()
+        at = peers + step
+        beside_copies.append(
+            push(place(step, over), place(step, over), c_send.at[at], c_recv.at[at], beside)
+        )
+        beside_copies[-1].start()
+    for copy in beside_copies:
+        copy.wait_recv()
+    for copy in along_copies + across_copies + beside_copies:
+        copy.wait_send()
+
+
 def gather_tokens(block):
-    return lax.all_gather(
-        lax.all_gather(block, "dp", axis=0, tiled=True), "mp", axis=1, tiled=True
-    )
+    peers = lax.axis_size("dp")
+    shape = (block.shape[0] * peers, block.shape[1] * 4)
+    dma = pltpu.SemaphoreType.DMA
+    return in_vmem(
+        functools.partial(gather_kernel, peers),
+        block,
+        jax.ShapeDtypeStruct(shape, block.dtype),
+        [dma((peers - 1,))] * 2 + [dma((peers,))] * 2 + [dma((2 * peers,))] * 2,
+        0,
+    )
+
+
+def exchange_kernel(peers, x_ref, o_ref, send, recv):
+    rows = x_ref.shape[0] // peers
+    row = lax.axis_index("dp")
+    along = mesh_partners(peers)[0]
+    greet(along)
+    own = pl.ds(pl.multiple_of(row * rows, rows), rows)
+    copies = []
+    for step in range(1, peers):
+        other = lax.rem(row + step, peers)
+        theirs = pl.ds(pl.multiple_of(other * rows, rows), rows)
+        copies.append(
+            push(
+                x_ref.at[theirs], o_ref.at[own], send.at[step - 1], recv.at[step - 1], along[step - 1]
+            )
+        )
+        copies[-1].start()
+    o_ref[own] = x_ref[own]
+    for copy in copies:
+        copy.wait()
 
 
 def exchange_rows(array):
-    return lax.all_to_all(array, "dp", 0, 0, tiled=True)
+    peers = lax.axis_size("dp")
+    return in_vmem(
+        functools.partial(exchange_kernel, peers),
+        array,
+        jax.ShapeDtypeStruct(array.shape, array.dtype),
+        [pltpu.SemaphoreType.DMA((peers - 1,))] * 2,
+        1 if array.shape[1] % 768 else 2,
+    )
+
+
+def spread_kernel(peers, x_ref, o_ref, send, recv):
+    rows = x_ref.shape[0]
+    row = lax.axis_index("dp")
+    along = mesh_partners(peers)[0]
+    greet(along)
+    own = pl.ds(pl.multiple_of(row * rows, rows), rows)
+    copies = [
+        push(x_ref, o_ref.at[own], send.at[step], recv.at[step], along[step])
+        for step in range(peers - 1)
+    ]
+    for copy in copies:
+        copy.start()
+    o_ref[own] = x_ref[...]
+    for copy in copies:
+        copy.wait()
 
 
 def gather_rows(array):
-    return lax.all_gather(array, "dp", axis=0, tiled=True)
+    peers = lax.axis_size("dp")
+    return in_vmem(
+        functools.partial(spread_kernel, peers),
+        array,
+        jax.ShapeDtypeStruct((array.shape[0] * peers, array.shape[1]), array.dtype),
+        [pltpu.SemaphoreType.DMA((peers - 1,))] * 2,
+        3,
+    )
+
+
+def scatter_kernel(
+    peers, x_ref, o_ref, came, passed, landed, c_send, c_recv, y_send, y_recv
+):
+    width = x_ref.shape[1] // 4
+    rows = x_ref.shape[0] // peers
+    col = lax.axis_index("mp")
+    _, across, beside = mesh_partners(peers)
+    greet([across, beside])
+    next_to = col + 1 - 2 * lax.rem(col, 2)
+    over = lax.rem(col + 2, 4)
+    over_next = lax.rem(next_to + 2, 4)
+
+    def piece(step, owner):
+        return (
+            pl.ds(step * rows, rows),
+            pl.ds(pl.multiple_of(owner * width, width), width),
+        )
+
+    far, near = [], []
+    for step in range(peers):
+        for slot, owner, copies in ((0, over_next, far), (1, next_to, near)):
+            at = slot * peers + step
+            copies.append(
+                push(
+                    x_ref.at[piece(step, owner)],
+                    came.at[slot, pl.ds(step * rows, rows)],
+                    c_send.at[at],
+                    c_recv.at[at],
+                    beside,
+                )
+            )
+            if slot == 0:
+                copies[-1].start()
+    for copy in near:
+        copy.start()
+    across_copies = []
+    for step in range(peers):
+        here = pl.ds(step * rows, rows)
+        far[step].wait_recv()
+        passed[here] = (
+            x_ref[piece(step, over)].astype(jnp.float32) + came[0, here].astype(jnp.float32)
+        ).astype(jnp.bfloat16)
+        across_copies.append(
+            push(passed.at[here], landed.at[here], y_send.at[step], y_recv.at[step], across)
+        )
+        across_copies[-1].start()
+    for step in range(peers):
+        here = pl.ds(step * rows, rows)
+        near[step].wait_recv()
+        across_copies[step].wait_recv()
+        o_ref[here] = (
+            x_ref[piece(step, col)].astype(jnp.float32)
+            + came[1, here].astype(jnp.float32)
+            + landed[here].astype(jnp.float32)
+        ).astype(jnp.bfloat16)
+    for copy in far + near + across_copies:
+        copy.wait_send()
 
 
 def scatter_features(array):
-    return lax.psum_scatter(array, "mp", scatter_dimension=1, tiled=True)
+    peers = lax.axis_size("dp")
+    shape = (array.shape[0], array.shape[1] // 4)
+    dma = pltpu.SemaphoreType.DMA
+    return in_vmem(
+        functools.partial(scatter_kernel, peers),
+        array,
+        jax.ShapeDtypeStruct(shape, array.dtype),
+        [
+            pltpu.VMEM((2,) + shape, jnp.bfloat16),
+            pltpu.VMEM(shape, jnp.bfloat16),
+            pltpu.VMEM(shape, jnp.bfloat16),
+        ]
+        + [dma((2 * peers,))] * 2
+        + [dma((peers,))] * 2,
+        4,
+    )
 
 
 def scatter_from_last(array):
@@ -401,7 +627,8 @@
 
 def section_step(*arrays):
     model_width = arrays[0].shape[2] * lax.axis_size("mp")
-    if arrays[4].shape[1] == model_width and lax.axis_size("dp") == 4:
+    sizes = tuple(lax.axis_size(axis) for axis in ("segment", "dp", "mp"))
+    if arrays[4].shape[1] == model_width and sizes == (2, 4, 4):
         return still_shards(*arrays)
     return shards(*arrays)
 

time: 500 us -> 362 us (0.72)
  Pallas kernels: 0 us -> 264 us
  blocking collectives: 196 us -> 5.06 us
  waiting for transfers between devices: 181 us -> 11 us
  other arithmetic: 25 us -> 10.7 us
  between operations: 14.2 us -> 1.22 us
  matrix products: 58.6 us -> 52.6 us
    pallas_call x0 -> x13, Pallas kernels: none -> 264 us  [in_vmem(): pl.pallas_call(kernel, out_shape=out_shape, in_specs=[pl.BlockSpec(memory...]
    all_to_all x6 -> x0, blocking collectives: 117 us -> none  [exchange_rows(): return lax.all_to_all(array, 'dp', 0, 0, tiled=True)]
    all_gather x3 -> x0, waiting for transfers between devices: 79.9 us -> none  [gather_tokens(): lax.all_gather(lax.all_gather(block, 'dp', axis=0, tiled=True), 'mp', axi...]
    all_gather x4 -> x0, blocking collectives: 73.9 us -> none  [the longest x3 58.2 us: gather_tokens(): lax.all_gather(block, 'dp', axis=0, tiled=True)]
    reduce_scatter x2 -> x0, waiting for transfers between devices: 72.3 us -> none  [scatter_features(): return lax.psum_scatter(array, 'mp', scatter_dimension=1, tiled=True)]
    all_to_all x1 -> x0, waiting for transfers between devices: 17.9 us -> none  [exchange_rows(): return lax.all_to_all(array, 'dp', 0, 0, tiled=True)]
  transfers between devices with their start and end apart: 8 -> 2, of which waited for: 8 -> 2; matrix products, arithmetic and copies ran while one was open for 1% -> 0% of each run, Pallas kernels for 0% -> 0%
where the time goes in v2:
time: 362 us
  Pallas kernels  264 us (73%)
  matrix products  52.6 us (15%)
  local copies, waits for them, and re-layouts  11.9 us (3%)
  waiting for transfers between devices  11 us (3%)
  other arithmetic  10.7 us (3%)
  starting transfers between devices  5.15 us (1%)
  blocking collectives  5.06 us (1%)
    pallas_call x13, Pallas kernels, in_vmem(): pl.pallas_call(kernel, out_shape=out_shape, in_specs=[pl.BlockSpec(memory...  264 us
    dot_general x1, matrix products, still_shards(): lax.dot_general(left_side, right_side, (((0,), (0,)), ((), ())), preferre...  17 us
    dot_general x3, matrix products, times_weights(): jnp.dot(left, weights, preferred_element_type=jnp.float32)  11.2 us
    ppermute x1, waiting for transfers between devices, still_shards(): own_d = lax.ppermute(own_d, 'segment', [(1, 0)])  7.5 us
  transfers between devices with their start and end apart: 2, of which 2 were waited for; matrix products, arithmetic and copies ran while one was open for 0% of the time, Pallas kernels for 0%

profile of v2, /device:TPU:0, one launch (start us, length us, event | category | flops | bytes accessed | tf_op | source)
XLA Modules:
  0.0 361.8 jit_solution(6149507185554280711)
XLA Ops:
  1.4 2.7 broadcast_select_fusion
  4.1 30.5 %shard_map.94 = bf16[512,3072]{1,0:T(8,128)(2,1)S(1)} custom-call(bf16[128,768]{1,0:T(8,128)(2,1)S(1)} %bitcast.110), custom_call_target="tpu_custom_call" | custom-call | tf_op jit(solution)/shard_map/pallas_call | solution.py:268
  35.1 1.0 fusion.11
  36.0 2.1 bitcast_convert_fusion
  38.1 3.7 %fusion.37.x_ref = bf16[512,512]{1,0:T(8,128)(2,1)S(1)} fusion(bf16[3072,512]{1,0:T(8,128)(2,1)} %bitcast_convert_fusion, bf16[512,3072]{1,0:T(8,128)(2,1)S(1)} %shard_map.94, f32[3072]{0:T(1024)S(1)} %bitcast.126, f32[512]{0:T(512)S(1)} %add_rsqrt_fusion.1, f32[512]{0:T(512)S(1)} %broadcast_multiply_fusion.1, pred[]{:T(512)S(6)} %eq.9), kind=kOutput, calls=%fused_computation.49 | convolution fusion | flops 1620312064 | bytes 6832129 | tf_op jit(solution)/shard_map/dot_general | solution.py:551
  41.9 15.8 %shard_map.95 = bf16[512,512]{1,0:T(8,128)(2,1)S(1)} custom-call(bf16[512,512]{1,0:T(8,128)(2,1)S(1)} %fusion.37.x_ref), custom_call_target="tpu_custom_call" | custom-call | tf_op jit(solution)/shard_map/pallas_call | solution.py:268
  57.8 1.0 fusion.174
  59.3 15.0 %shard_map.96 = bf16[512,512]{1,0:T(8,128)(2,1)S(1)} custom-call(bf16[128,512]{1,0:T(8,128)(2,1)S(1)} %bitcast.108), custom_call_target="tpu_custom_call" | custom-call | tf_op jit(solution)/shard_map/pallas_call | solution.py:268
  74.4 3.7 %convolution_convert_fusion.1.x_ref = bf16[512,3072]{1,0:T(8,128)(2,1)S(1)} fusion(bf16[512,512]{1,0:T(8,128)(2,1)S(1)} %shard_map.96, bf16[3072,512]{1,0:T(8,128)(2,1)} %bitcast_convert_fusion), kind=kOutput, calls=%fused_computation.28 | convolution fusion | flops 1612185600 | bytes 6815744 | tf_op jit(solution)/shard_map/dot_general | solution.py:555
  78.1 20.1 %shard_map.97.x_ref = bf16[512,768]{1,0:T(8,128)(2,1)S(1)} custom-call(bf16[512,3072]{1,0:T(8,128)(2,1)S(1)} %convolution_convert_fusion.1.x_ref), custom_call_target="tpu_custom_call" | custom-call | tf_op jit(solution)/shard_map/pallas_call | solution.py:268
  98.2 19.5 %shard_map.98 = bf16[512,768]{1,0:T(8,128)(2,1)S(1)} custom-call(bf16[512,768]{1,0:T(8,128)(2,1)S(1)} %shard_map.97.x_ref), custom_call_target="tpu_custom_call" | custom-call | tf_op jit(solution)/shard_map/pallas_call | solution.py:268
  117.8 3.6 %collective-permute-start = (bf16[128,768]{1,0:T(8,128)(2,1)S(1)}, bf16[128,768]{1,0:T(8,128)(2,1)S(1)}, u32[]{:S(2)}, u32[]{:S(2)}) collective-permute-start(bf16[128,768]{1,0:T(8,128)(2,1)S(1)} %fusion.73), channel_id=1, source_target_pairs={{0,16},{1,17},{2,18},{3,19},{4,20},{5,21},{6,22},{7,23},{8,24},{9,... | collective-permute-start | bytes 589832 | tf_op jit(solution)/shard_map/ppermute | solution.py:589
  121.5 3.5 collective-permute-done.x_ref
  125.0 29.7 %shard_map.99 = bf16[512,3072]{1,0:T(8,128)(2,1)S(1)} custom-call(bf16[128,768]{1,0:T(8,128)(2,1)S(1)} %collective-permute-done.x_ref), custom_call_target="tpu_custom_call" | custom-call | tf_op jit(solution)/shard_map/pallas_call | solution.py:268
  155.2 1.0 fusion.8
  156.2 3.7 %convolution_convert_fusion.3.x_ref = bf16[512,512]{1,0:T(8,128)(2,1)S(1)} fusion(bf16[3072,512]{1,0:T(8,128)(2,1)} %bitcast_convert_fusion, bf16[512,3072]{1,0:T(8,128)(2,1)} %copy-done, bf16[512,3072]{1,0:T(8,128)(2,1)S(1)} %shard_map.99, f32[512]{0:T(512)S(1)} %add_rsqrt_fusion, f32[512]{0:T(512)S(1)} %broadcast_multiply_fusion, f32[3072]{0:T(1024)S(1)} %bitcast.127, ...), kind=kOutput, calls=%fused_computation.51 | convolution fusion | flops 1620312064 | bytes 9977857 | tf_op jit(solution)/shard_map/dot_general | solution.py:551
  159.9 17.2 %shard_map.100 = bf16[512,512]{1,0:T(8,128)(2,1)S(1)} custom-call(bf16[512,512]{1,0:T(8,128)(2,1)S(1)} %convolution_convert_fusion.3.x_ref), custom_call_target="tpu_custom_call" | custom-call | tf_op jit(solution)/shard_map/pallas_call | solution.py:268
  177.1 0.7 fusion.172
  177.8 0.9 reshape.142
  178.8 1.6 reshape.141
  181.0 0.9 reshape.143
  182.0 0.9 fusion.85
  182.9 2.5 fusion.179
  185.4 2.0 fusion.57
  187.4 1.4 fusion.54
  188.8 1.5 fusion.56
  190.3 2.2 fusion.53
  192.8 1.1 copy.53
  193.9 1.0 copy.49
  195.1 15.0 %shard_map.101 = bf16[512,512]{1,0:T(8,128)(2,1)S(1)} custom-call(bf16[512,512]{1,0:T(8,128)(2,1)S(1)} %pad_maximum_fusion.x_ref), custom_call_target="tpu_custom_call" | custom-call | tf_op jit(solution)/shard_map/pallas_call | solution.py:268
  210.9 1.8 convolution_convert_fusion.x_ref
  212.7 20.6 %shard_map.102.x_ref = bf16[512,768]{1,0:T(8,128)(2,1)S(1)} custom-call(bf16[512,3072]{1,0:T(8,128)(2,1)S(1)} %convolution_convert_fusion.x_ref), custom_call_target="tpu_custom_call" | custom-call | tf_op jit(solution)/shard_map/pallas_call | solution.py:268
  233.4 19.3 %shard_map.103 = bf16[512,768]{1,0:T(8,128)(2,1)S(1)} custom-call(bf16[512,768]{1,0:T(8,128)(2,1)S(1)} %shard_map.102.x_ref), custom_call_target="tpu_custom_call" | custom-call | tf_op jit(solution)/shard_map/pallas_call | solution.py:268
  253.5 5.1 %all-gather.1 = f32[4,2,128]{2,1,0:T(2,128)S(1)} all-gather(f32[1,2,128]{2,1,0:T(2,128)S(1)} %maximum_bitcast_fusion), channel_id=2, replica_groups=mesh['segment'=2,'dp'=4,'mp'=4] {'mp'}, dimensions={0}, use_global_device_ids=true | all-gather | bytes 5120 | tf_op jit(solution)/shard_map/all_gather | solution.py:494
  258.6 1.3 fusion.74
  259.9 1.5 collective-permute-start.1
  261.4 7.5 %collective-permute-done.1.x_ref = bf16[128,768]{1,0:T(8,128)(2,1)S(1)} collective-permute-done((bf16[128,768]{1,0:T(8,128)(2,1)S(1)}, bf16[128,768]{1,0:T(8,128)(2,1)S(1)}, u32[]{:S(2)}, u32[]{:S(2)}) %collective-permute-start.1) | collective-permute-done | bytes 196640 | tf_op jit(solution)/shard_map/ppermute | solution.py:609
  268.9 30.7 %shard_map.104 = bf16[512,3072]{1,0:T(8,128)(2,1)S(1)} custom-call(bf16[128,768]{1,0:T(8,128)(2,1)S(1)} %collective-permute-done.1.x_ref), custom_call_target="tpu_custom_call" | custom-call | tf_op jit(solution)/shard_map/pallas_call | solution.py:268
  299.7 1.7 copy-done.1
  301.4 3.7 %convolution_convert_fusion.2.x_ref = bf16[512,512]{1,0:T(8,128)(2,1)S(1)} fusion(bf16[512,3072]{1,0:T(8,128)(2,1)S(1)} %shard_map.104, bf16[3072,512]{1,0:T(8,128)(2,1)} %bitcast_convert_fusion), kind=kOutput, calls=%fused_computation.50 | convolution fusion | flops 1610874880 | bytes 6815744 | tf_op jit(solution)/shard_map/dot_general | solution.py:551
  305.1 15.8 %shard_map.105 = bf16[512,512]{1,0:T(8,128)(2,1)S(1)} custom-call(bf16[512,512]{1,0:T(8,128)(2,1)S(1)} %convolution_convert_fusion.2.x_ref), custom_call_target="tpu_custom_call" | custom-call | tf_op jit(solution)/shard_map/pallas_call | solution.py:268
  321.6 1.8 fusion.80
  323.4 1.4 fusion.59
  324.8 1.5 fusion.55
  326.3 2.2 fusion.58
  328.5 1.0 copy.63
  329.7 15.0 %shard_map.106 = bf16[512,512]{1,0:T(8,128)(2,1)S(1)} custom-call(bf16[512,512]{1,0:T(8,128)(2,1)S(1)} %pad_maximum_fusion.1.x_ref), custom_call_target="tpu_custom_call" | custom-call | tf_op jit(solution)/shard_map/pallas_call | solution.py:268
  344.8 17.0 %fusion.36 = (f32[1,3072,512]{2,1,0:T(8,128)}, f32[1,3072,512]{2,1,0:T(8,128)}, f32[1,3072,512]{2,1,0:T(8,128)}) fusion(f32[1,3072,512]{2,1,0:T(8,128)} %param.13, f32[1,3072,512]{2,1,0:T(8,128)} %param.12, f32[1,3072,512]{2,1,0:T(8,128)} %param.11, bf16[512,512]{1,0:T(8,128)(2,1)S(1)} %shard_map.106, bf16[512,512]{1,0:T(8,128)(2,1)} %copy-done.2, ...), kind=kOutput, calls=%fused_computation.47 | convolution fusion | flops 1654915072 | bytes 48254976 | tf_op jit(solution)/shard_map/dot_general | solution.py:619
  (74 shorter events, 6.1 us)
Async XLA Ops:
  1.4 34.7 %copy-start.3 = (f32[1,3072,512]{2,1,0:T(8,128)S(1)}, f32[1,3072,512]{2,1,0:T(8,128)}, u32[]{:S(2)}) copy-start(f32[1,3072,512]{2,1,0:T(8,128)} %param.11) | copy-start | bytes 18874372
  34.6 3.6 copy-start
  35.1 3.1 copy-start.14
  57.7 20.4 %copy-start.10 = (bf16[8,16,4,128]{3,2,1,0:T(4,128)(2,1)}, bf16[8,16,4,128]{3,2,1,0:T(4,128)(2,1)S(1)}, u32[]{:S(2)}) copy-start(bf16[8,16,4,128]{3,2,1,0:T(4,128)(2,1)S(1)} %reshape.137) | copy-start | bytes 393220
  57.8 20.3 %copy-start.11 = (bf16[8,16,4,128]{3,2,1,0:T(4,128)(2,1)}, bf16[8,16,4,128]{3,2,1,0:T(4,128)(2,1)S(1)}, u32[]{:S(2)}) copy-start(bf16[8,16,4,128]{3,2,1,0:T(4,128)(2,1)S(1)} %reshape.138) | copy-start | bytes 393220
  57.8 1.5 copy-start.8
  58.8 19.3 %copy-start.15 = (f32[8,4,16]{2,1,0:T(4,128)}, f32[8,4,16]{2,1,0:T(4,128)S(1)}, u32[]{:S(2)}) copy-start(f32[8,4,16]{2,1,0:T(4,128)S(1)} %get-tuple-element.21) | copy-start | bytes 6148
  117.8 7.2 %collective-permute-start = (bf16[128,768]{1,0:T(8,128)(2,1)S(1)}, bf16[128,768]{1,0:T(8,128)(2,1)S(1)}, u32[]{:S(2)}, u32[]{:S(2)}) collective-permute-start(bf16[128,768]{1,0:T(8,128)(2,1)S(1)} %fusion.73), channel_id=1, source_target_pairs={{0,16},{1,17},{2,18},{3,19},{4,20},{5,21},{6,22},{7,23},{8,24},{9,... | collective-permute-start | bytes 589832 | tf_op jit(solution)/shard_map/ppermute | solution.py:589
  156.1 3.8 %copy-start.12 = (f32[512]{0:T(512)}, f32[512]{0:T(512)S(1)}, u32[]{:S(2)}) copy-start(f32[512]{0:T(512)S(1)} %add_rsqrt_fusion) | copy-start | bytes 6148
  192.6 18.3 %copy-start.6 = (bf16[3072,512]{1,0:T(8,128)(2,1)S(1)}, bf16[3072,512]{1,0:T(8,128)(2,1)}, u32[]{:S(2)}) copy-start(bf16[3072,512]{1,0:T(8,128)(2,1)} %bitcast_convert_fusion) | copy-start | bytes 9437188
  210.1 0.8 copy-start.2
  210.4 42.3 %copy-start.4 = (f32[128,3072]{1,0:T(8,128)}, f32[128,3072]{1,0:T(8,128)S(1)}, u32[]{:S(2)}) copy-start(f32[128,3072]{1,0:T(8,128)S(1)} %get-tuple-element.11) | copy-start | bytes 4718596
  212.7 45.9 %copy-start.7 = (bf16[8,16,768]{2,1,0:T(8,128)(2,1)S(1)}, bf16[8,16,768]{2,1,0:T(8,128)(2,1)}, u32[]{:S(2)}) copy-start(bf16[8,16,768]{2,1,0:T(8,128)(2,1)} %param.9) | copy-start | bytes 589828
  252.8 0.7 copy-start.5
  259.9 9.0 %collective-permute-start.1 = (bf16[128,768]{1,0:T(8,128)(2,1)S(1)}, bf16[128,768]{1,0:T(8,128)(2,1)S(1)}, u32[]{:S(2)}, u32[]{:S(2)}) collective-permute-start(bf16[128,768]{1,0:T(8,128)(2,1)S(1)} %fusion.74), channel_id=1, source_target_pairs={{16,0},{17,1},{18,2},{19,3},{20,4},{21,5},{22,6},{23,7},{24,8},{25... | collective-permute-start | bytes 589832 | tf_op jit(solution)/shard_map/ppermute | solution.py:609
  299.6 1.7 copy-start.1
  301.4 20.2 %copy-start.9 = (bf16[8,16,4,128]{3,2,1,0:T(4,128)(2,1)S(1)}, bf16[8,16,4,128]{3,2,1,0:T(4,128)(2,1)}, u32[]{:S(2)}) copy-start(bf16[8,16,4,128]{3,2,1,0:T(4,128)(2,1)} %copy-done.8) | copy-start | bytes 393220
  305.1 39.7 %copy-start.13 = (f32[512]{0:T(512)S(1)}, f32[512]{0:T(512)}, u32[]{:S(2)}) copy-start(f32[512]{0:T(512)} %copy-done.12) | copy-start | bytes 6148

commit v3 on v2

--- a/solution.py
+++ b/solution.py
@@ -285,65 +285,116 @@
     return (along, across, beside)
 
 
-def gather_kernel(peers, x_ref, o_ref, z_send, z_recv, y_send, y_recv, c_send, c_recv):
+def gather_kernel(peers, crossing, x_ref, o_ref, *scratch):
+    z_send, z_recv, y_send, y_recv, c_send, c_recv = scratch[:6]
     rows, width = x_ref.shape
     row, col = lax.axis_index("dp"), lax.axis_index("mp")
-    along, across, beside = mesh_partners(peers)
-    greet(along + [across, beside])
-
-    def place(step, owner):
-        source = lax.rem(row - step + peers, peers)
+    _, across, beside = mesh_partners(peers)
+    lines = ({"dp": lax.rem(row + 1, peers)}, {"dp": lax.rem(row + peers - 1, peers)})
+    opposite = {"segment": 1 - lax.axis_index("segment")}
+    greet(list(lines) + [across, beside] + ([opposite] if crossing else []))
+    over = lax.rem(col + 2, 4)
+    held = x_ref
+    if crossing:
+        held, x_send, x_recv = scratch[6:]
+        entering = push(x_ref, held, x_send, x_recv, opposite)
+        entering.start()
+        entering.wait_recv()
+
+    def source_of(side, away):
+        return row - away if side == 0 else row + away
+
+    def there(side, away):
+        return row >= away if side == 0 else row + away < peers
+
+    def passes(side):
+        return row < peers - 1 if side == 0 else row > 0
+
+    def slot_of(side, away):
+        return 0 if away == 0 else side * (peers - 1) + away
+
+    def place(side, away, owner):
         return o_ref.at[
-            pl.ds(pl.multiple_of(source * rows, rows), rows),
+            pl.ds(pl.multiple_of(source_of(side, away) * rows, rows), rows),
             pl.ds(pl.multiple_of(owner * width, width), width),
         ]
 
-    over = lax.rem(col + 2, 4)
-    along_copies = [
-        push(x_ref, place(0, col), z_send.at[step], z_recv.at[step], along[step])
-        for step in range(peers - 1)
-    ]
-    for copy in along_copies:
-        copy.start()
-    across_copies, beside_copies = [], []
-    for step in range(peers):
-        source = x_ref
-        if step > 0:
-            along_copies[step - 1].wait_recv()
-            source = place(step, col)
-        across_copies.append(
-            push(source, place(step, col), y_send.at[step], y_recv.at[step], across)
-        )
-        across_copies[-1].start()
-        beside_copies.append(
-            push(source, place(step, col), c_send.at[step], c_recv.at[step], beside)
-        )
-        beside_copies[-1].start()
+    def block(side, away):
+        return held if away == 0 else place(side, away, col)
+
+    def onward(side, away):
+        at = side * (peers - 1) + away
+        target = place(side, away, col)
+        return push(block(side, away), target, z_send.at[at], z_recv.at[at], lines[side])
+
+    def sideways(side, away):
+        at = slot_of(side, away)
+        target = place(side, away, col)
+        return push(block(side, away), target, y_send.at[at], y_recv.at[at], across)
+
+    def inward(side, away, both):
+        at = slot_of(side, away) + both * (2 * peers - 1)
+        target = place(side, away, over if both else col)
+        source = target if both else block(side, away)
+        return push(source, target, c_send.at[at], c_recv.at[at], beside)
+
+    every = [(0, 0)] + [(side, away) for away in range(1, peers) for side in (0, 1)]
+
+    def where_there(side, away, action):
+        if away == 0:
+            action(side, away)
+        else:
+            pl.when(there(side, away))(functools.partial(action, side, away))
+
+    def arrive(side, away):
+        if away > 0:
+            onward(side, away - 1).wait_recv()
+        for way in (0, 1) if away == 0 else (side,):
+            if away < peers - 1:
+                pl.when(passes(way))(functools.partial(lambda w: onward(w, away).start(), way))
+        sideways(side, away).start()
+        inward(side, away, 0).start()
+
+    def relay(side, away):
+        sideways(side, away).wait_recv()
+        inward(side, away, 1).start()
+
+    def finish(side, away):
+        inward(side, away, 0).wait_recv()
+        inward(side, away, 1).wait_recv()
+        for way in (0, 1) if away == 0 else (side,):
+            if away < peers - 1:
+                pl.when(passes(way))(functools.partial(lambda w: onward(w, away).wait_send(), way))
+        sideways(side, away).wait_send()
+        inward(side, away, 0).wait_send()
+        inward(side, away, 1).wait_send()
+
+    for side, away in every:
+        where_there(side, away, arrive)
     own_rows = pl.ds(pl.multiple_of(row * rows, rows), rows)
-    o_ref[own_rows, pl.ds(pl.multiple_of(col * width, width), width)] = x_ref[...]
-    for step in range(peers):
-        across_copies[step].wait_recv()
-        at = peers + step
-        beside_copies.append(
-            push(place(step, over), place(step, over), c_send.at[at], c_recv.at[at], beside)
-        )
-        beside_copies[-1].start()
-    for copy in beside_copies:
-        copy.wait_recv()
-    for copy in along_copies + across_copies + beside_copies:
-        copy.wait_send()
-
-
-def gather_tokens(block):
+    o_ref[own_rows, pl.ds(pl.multiple_of(col * width, width), width)] = held[...]
+    for side, away in every:
+        where_there(side, away, relay)
+    for side, away in every:
+        where_there(side, away, finish)
+    if crossing:
+        entering.wait_send()
+
+
+def gather_tokens(block, crossing=False):
     peers = lax.axis_size("dp")
     shape = (block.shape[0] * peers, block.shape[1] * 4)
     dma = pltpu.SemaphoreType.DMA
+    scratch = [dma((2 * peers - 2,))] * 2 + [dma((2 * peers - 1,))] * 2
+    scratch += [dma((4 * peers - 2,))] * 2
+    if crossing:
+        scratch += [pltpu.VMEM(block.shape, block.dtype), dma, dma]
     return in_vmem(
-        functools.partial(gather_kernel, peers),
+        functools.partial(gather_kernel, peers, crossing),
         block,
         jax.ShapeDtypeStruct(shape, block.dtype),
-        [dma((peers - 1,))] * 2 + [dma((peers,))] * 2 + [dma((2 * peers,))] * 2,
-        0,
+        scratch,
+        5 if crossing else 0,
     )
 
 
@@ -379,31 +430,78 @@
     )
 
 
-def spread_kernel(peers, x_ref, o_ref, send, recv):
+def to_last_kernel(peers, x_ref, o_ref, send, recv):
     rows = x_ref.shape[0]
     row = lax.axis_index("dp")
-    along = mesh_partners(peers)[0]
-    greet(along)
-    own = pl.ds(pl.multiple_of(row * rows, rows), rows)
-    copies = [
-        push(x_ref, o_ref.at[own], send.at[step], recv.at[step], along[step])
-        for step in range(peers - 1)
-    ]
-    for copy in copies:
-        copy.start()
-    o_ref[own] = x_ref[...]
-    for copy in copies:
-        copy.wait()
+    greet(mesh_partners(peers)[0])
+
+    def copy_from(source):
+        return push(
+            x_ref,
+            o_ref.at[pl.ds(source * rows, rows)],
+            send.at[source],
+            recv.at[source],
+            {"dp": peers - 1},
+        )
+
+    for source in range(peers - 1):
+
+        @pl.when(row == source)
+        def _():
+            copy_from(source).start()
+            o_ref[...] = jnp.zeros_like(o_ref)
+            copy_from(source).wait_send()
+
+    @pl.when(row == peers - 1)
+    def _():
+        o_ref[pl.ds((peers - 1) * rows, rows)] = x_ref[...]
+        for source in range(peers - 1):
+            copy_from(source).wait_recv()
 
 
 def gather_rows(array):
     peers = lax.axis_size("dp")
     return in_vmem(
-        functools.partial(spread_kernel, peers),
+        functools.partial(to_last_kernel, peers),
         array,
         jax.ShapeDtypeStruct((array.shape[0] * peers, array.shape[1]), array.dtype),
         [pltpu.SemaphoreType.DMA((peers - 1,))] * 2,
         3,
+    )
+
+
+def from_last_kernel(peers, x_ref, o_ref, send, recv):
+    rows = o_ref.shape[0]
+    row = lax.axis_index("dp")
+    greet(mesh_partners(peers)[0])
+    copies = [
+        push(
+            x_ref.at[pl.ds(target * rows, rows)], o_ref, send.at[target], recv, {"dp": target}
+        )
+        for target in range(peers - 1)
+    ]
+
+    @pl.when(row == peers - 1)
+    def _():
+        for copy in copies:
+            copy.start()
+        o_ref[...] = x_ref[pl.ds((peers - 1) * rows, rows)]
+        for copy in copies:
+            copy.wait_send()
+
+    @pl.when(row < peers - 1)
+    def _():
+        copies[0].wait_recv()
+
+
+def scatter_from_last(array):
+    peers = lax.axis_size("dp")
+    return in_vmem(
+        functools.partial(from_last_kernel, peers),
+        array,
+        jax.ShapeDtypeStruct((array.shape[0] // peers, array.shape[1]), array.dtype),
+        [pltpu.SemaphoreType.DMA((peers - 1,)), pltpu.SemaphoreType.DMA],
+        6 if array.shape[1] % 768 else 7,
     )
 
 
@@ -485,11 +583,6 @@
     )
 
 
-def scatter_from_last(array):
-    rows = array.shape[0] // lax.axis_size("dp")
-    return exchange_rows(array)[-rows:]
-
-
 def row_sums(array):
     return jnp.sum(lax.all_gather(array, "mp", axis=0), axis=0)
 
@@ -586,9 +679,8 @@
         scatter_features(times_weights_t(gather_rows(attended0), weights))
     )
     own_out = (own_input.astype(jnp.float32) + mixed.astype(jnp.float32)).astype(jnp.bfloat16)
-    own_out = lax.ppermute(own_out, "segment", [(0, 1)])
-
-    middle = gather_tokens(own_out)
+
+    middle = gather_tokens(own_out, True)
     left_second = jnp.where(holds_out, entered, norm_forward(middle, norm_scale)[0])
     q1, k1, v1, da1 = parts_of(exchange_rows(times_weights(left_second, weights)))
     probs1, attended1 = attend(q1, k1, v1, length)
@@ -606,9 +698,8 @@
     ) * (1.0 / model_width)
     inner = scaled - sums[0][:, None] - standard * sums[1][:, None]
     own_d = (own_grad.astype(jnp.float32) + inner * inverse_dev).astype(jnp.bfloat16)
-    own_d = lax.ppermute(own_d, "segment", [(1, 0)])
-
-    returned = gather_tokens(own_d)
+
+    returned = gather_tokens(own_d, True)
     da0 = scatter_from_last(times_weights(returned, weights))
     grads0 = attend_back(q0, k0, v0, probs0, da0, length)
     right_first = exchange_rows(jnp.concatenate(grads0 + (attended0,), axis=0))

time: 362 us -> 324 us (0.90)
  Pallas kernels: 264 us -> 242 us
  waiting for transfers between devices: 11 us -> 0 us
  starting transfers between devices: 5.15 us -> 0 us
    pallas_call x13, Pallas kernels: 264 us -> 242 us  [in_vmem(): pl.pallas_call(kernel, out_shape=out_shape, in_specs=[pl.BlockSpec(memory...]
    ppermute x2 -> x0, waiting for transfers between devices: 11 us -> none  [the longest x1 7.5 us: still_shards(): own_d = lax.ppermute(own_d, 'segment', [(1, 0)])]
    ppermute x2 -> x0, starting transfers between devices: 5.15 us -> none  [the longest x1 3.63 us: still_shards(): own_out = lax.ppermute(own_out, 'segment', [(0, 1)])]
    dot_general x3, matrix products: 11.2 us -> 7.39 us  [times_weights(): jnp.dot(left, weights, preferred_element_type=jnp.float32)]
  transfers between devices with their start and end apart: 2 -> 0, of which waited for: 2 -> 0; matrix products, arithmetic and copies ran while one was open for 0% -> 0% of each run, Pallas kernels for 0% -> 0%
where the time goes in v3:
time: 324 us; the launch traced here: 323 us
  Pallas kernels  242 us (75%)
  matrix products  49.5 us (15%)
  local copies, waits for them, and re-layouts  14.9 us (5%)
  other arithmetic  10.2 us (3%)
  blocking collectives  5.06 us (2%)
    pallas_call x13, Pallas kernels, in_vmem(): pl.pallas_call(kernel, out_shape=out_shape, in_specs=[pl.BlockSpec(memory...  242 us
    dot_general x1, matrix products, still_shards(): lax.dot_general(left_side, right_side, (((0,), (0,)), ((), ())), preferre...  17 us
    dot_general x3, matrix products, times_weights(): jnp.dot(left, weights, preferred_element_type=jnp.float32)  7.39 us

profile of v3, /device:TPU:0, one launch (start us, length us, event | category | flops | bytes accessed | tf_op | source)
XLA Modules:
  0.0 322.5 jit_solution(15219047593727395566)
XLA Ops:
  0.7 0.9 dynamic-slice_reduce_fusion
  1.5 0.9 convert_element_type.141
  2.4 2.6 broadcast_select_fusion
  5.0 27.0 %shard_map.94 = bf16[512,3072]{1,0:T(8,128)(2,1)S(1)} custom-call(bf16[128,768]{1,0:T(8,128)(2,1)S(1)} %bitcast.110), custom_call_target="tpu_custom_call" | custom-call | tf_op jit(solution)/shard_map/pallas_call | solution.py:268
  32.6 1.0 fusion.11
  34.0 1.7 copy-done.7
  35.6 1.8 fusion.37.x_ref
  37.5 13.0 %shard_map.95 = bf16[512,512]{1,0:T(8,128)(2,1)S(1)} custom-call(bf16[512,512]{1,0:T(8,128)(2,1)S(1)} %fusion.37.x_ref), custom_call_target="tpu_custom_call" | custom-call | tf_op jit(solution)/shard_map/pallas_call | solution.py:268
  50.7 1.0 fusion.174
  52.2 6.9 %shard_map.96 = bf16[512,512]{1,0:T(8,128)(2,1)S(1)} custom-call(bf16[128,512]{1,0:T(8,128)(2,1)S(1)} %bitcast.108), custom_call_target="tpu_custom_call" | custom-call | tf_op jit(solution)/shard_map/pallas_call | solution.py:268
  59.1 3.7 %convolution_convert_fusion.1.x_ref = bf16[512,3072]{1,0:T(8,128)(2,1)S(1)} fusion(bf16[512,512]{1,0:T(8,128)(2,1)S(1)} %shard_map.96, bf16[3072,512]{1,0:T(8,128)(2,1)} %copy-done.7), kind=kOutput, calls=%fused_computation.28 | convolution fusion | flops 1612185600 | bytes 6815744 | tf_op jit(solution)/shard_map/dot_general | solution.py:648
  62.8 20.1 %shard_map.97.x_ref = bf16[512,768]{1,0:T(8,128)(2,1)S(1)} custom-call(bf16[512,3072]{1,0:T(8,128)(2,1)S(1)} %convolution_convert_fusion.1.x_ref), custom_call_target="tpu_custom_call" | custom-call | tf_op jit(solution)/shard_map/pallas_call | solution.py:268
  83.0 13.9 %shard_map.98 = bf16[128,768]{1,0:T(8,128)(2,1)S(1)} custom-call(bf16[512,768]{1,0:T(8,128)(2,1)S(1)} %shard_map.97.x_ref), custom_call_target="tpu_custom_call" | custom-call | tf_op jit(solution)/shard_map/pallas_call | solution.py:268
  96.9 38.4 %shard_map.99 = bf16[512,3072]{1,0:T(8,128)(2,1)S(1)} custom-call(bf16[128,768]{1,0:T(8,128)(2,1)S(1)} %fusion.73.x_ref), custom_call_target="tpu_custom_call" | custom-call | tf_op jit(solution)/shard_map/pallas_call | solution.py:268
  136.6 1.0 fusion.8
  137.6 1.8 convolution_convert_fusion.3.x_ref
  139.4 13.0 %shard_map.100 = bf16[512,512]{1,0:T(8,128)(2,1)S(1)} custom-call(bf16[512,512]{1,0:T(8,128)(2,1)S(1)} %convolution_convert_fusion.3.x_ref), custom_call_target="tpu_custom_call" | custom-call | tf_op jit(solution)/shard_map/pallas_call | solution.py:268
  152.4 0.7 fusion.172
  153.2 0.9 reshape.142
  154.1 1.6 reshape.141
  156.4 0.9 reshape.143
  157.3 0.9 fusion.85
  158.2 2.5 fusion.179
  160.7 2.0 fusion.57
  162.8 1.0 copy.53
  163.7 2.0 fusion.54
  165.8 1.5 fusion.56
  167.3 2.2 fusion.53
  169.5 1.1 copy.49
  170.7 1.0 copy.56
  171.8 14.0 %shard_map.101 = bf16[512,512]{1,0:T(8,128)(2,1)S(1)} custom-call(bf16[512,512]{1,0:T(8,128)(2,1)S(1)} %pad_maximum_fusion.x_ref), custom_call_target="tpu_custom_call" | custom-call | tf_op jit(solution)/shard_map/pallas_call | solution.py:268
  185.8 0.9 multiply_reduce_fusion
  186.8 1.8 convolution_convert_fusion.x_ref
  188.7 20.1 %shard_map.102.x_ref = bf16[512,768]{1,0:T(8,128)(2,1)S(1)} custom-call(bf16[512,3072]{1,0:T(8,128)(2,1)S(1)} %convolution_convert_fusion.x_ref), custom_call_target="tpu_custom_call" | custom-call | tf_op jit(solution)/shard_map/pallas_call | solution.py:268
  208.8 18.7 %shard_map.103 = bf16[512,768]{1,0:T(8,128)(2,1)S(1)} custom-call(bf16[512,768]{1,0:T(8,128)(2,1)S(1)} %shard_map.102.x_ref), custom_call_target="tpu_custom_call" | custom-call | tf_op jit(solution)/shard_map/pallas_call | solution.py:268
  228.3 5.1 %all-gather.1 = f32[4,2,128]{2,1,0:T(2,128)S(1)} all-gather(f32[1,2,128]{2,1,0:T(2,128)S(1)} %maximum_bitcast_fusion), channel_id=2, replica_groups=mesh['segment'=2,'dp'=4,'mp'=4] {'mp'}, dimensions={0}, use_global_device_ids=true | all-gather | bytes 5120 | tf_op jit(solution)/shard_map/all_gather | solution.py:587
  233.4 1.3 fusion.74.x_ref
  234.7 32.5 %shard_map.104 = bf16[512,3072]{1,0:T(8,128)(2,1)S(1)} custom-call(bf16[128,768]{1,0:T(8,128)(2,1)S(1)} %fusion.74.x_ref), custom_call_target="tpu_custom_call" | custom-call | tf_op jit(solution)/shard_map/pallas_call | solution.py:268
  267.2 1.7 copy-done.2
  268.9 3.7 %convolution_convert_fusion.2.x_ref = bf16[512,512]{1,0:T(8,128)(2,1)S(1)} fusion(bf16[512,3072]{1,0:T(8,128)(2,1)S(1)} %shard_map.104, bf16[3072,512]{1,0:T(8,128)(2,1)} %copy-done.7), kind=kOutput, calls=%fused_computation.50 | convolution fusion | flops 1610874880 | bytes 6815744 | tf_op jit(solution)/shard_map/dot_general | solution.py:644
  272.7 8.2 %shard_map.105 = bf16[128,512]{1,0:T(8,128)(2,1)S(1)} custom-call(bf16[512,512]{1,0:T(8,128)(2,1)S(1)} %convolution_convert_fusion.2.x_ref), custom_call_target="tpu_custom_call" | custom-call | tf_op jit(solution)/shard_map/pallas_call | solution.py:268
  281.6 1.8 fusion.80
  283.4 1.4 fusion.59
  284.8 1.5 fusion.55
  286.4 2.2 fusion.58
  288.5 1.0 copy.63
  289.7 15.8 %shard_map.106 = bf16[512,512]{1,0:T(8,128)(2,1)S(1)} custom-call(bf16[512,512]{1,0:T(8,128)(2,1)S(1)} %pad_maximum_fusion.1.x_ref), custom_call_target="tpu_custom_call" | custom-call | tf_op jit(solution)/shard_map/pallas_call | solution.py:268
  305.5 17.0 %fusion.36 = (f32[1,3072,512]{2,1,0:T(8,128)}, f32[1,3072,512]{2,1,0:T(8,128)}, f32[1,3072,512]{2,1,0:T(8,128)}) fusion(f32[1,3072,512]{2,1,0:T(8,128)} %param.13, f32[1,3072,512]{2,1,0:T(8,128)} %param.12, f32[1,3072,512]{2,1,0:T(8,128)} %param.11, bf16[512,512]{1,0:T(8,128)(2,1)S(1)} %shard_map.106, bf16[512,512]{1,0:T(8,128)(2,1)} %copy-done.3, ...), kind=kOutput, calls=%fused_computation.47 | convolution fusion | flops 1654915072 | bytes 48254976 | tf_op jit(solution)/shard_map/dot_general | solution.py:710
  (75 shorter events, 5.5 us)
Async XLA Ops:
  0.6 32.9 %copy-start.4 = (f32[1,3072,512]{2,1,0:T(8,128)S(1)}, f32[1,3072,512]{2,1,0:T(8,128)}, u32[]{:S(2)}) copy-start(f32[1,3072,512]{2,1,0:T(8,128)} %param.11) | copy-start | bytes 18874372
  32.1 1.9 copy-start
  32.6 3.1 copy-start.17
  34.0 1.7 copy-start.7
  50.6 1.1 copy-start.13
  50.6 1.6 copy-start.14
  50.7 1.5 copy-start.11
  51.7 11.2 %copy-start.18 = (f32[8,4,16]{2,1,0:T(4,128)}, f32[8,4,16]{2,1,0:T(4,128)S(1)}, u32[]{:S(2)}) copy-start(f32[8,4,16]{2,1,0:T(4,128)S(1)} %get-tuple-element.21) | copy-start | bytes 6148
  82.9 54.6 %copy-start.1 = (bf16[512,3072]{1,0:T(8,128)(2,1)S(1)}, bf16[512,3072]{1,0:T(8,128)(2,1)}, u32[]{:S(2)}) copy-start(bf16[512,3072]{1,0:T(8,128)(2,1)} %copy-done) | copy-start | bytes 9437188
  83.0 54.6 %copy-start.8 = (bf16[3072,512]{1,0:T(8,128)(2,1)S(1)}, bf16[3072,512]{1,0:T(8,128)(2,1)}, u32[]{:S(2)}) copy-start(bf16[3072,512]{1,0:T(8,128)(2,1)} %copy-done.7) | copy-start | bytes 9437188
  137.5 1.9 copy-start.15
  169.5 17.3 %copy-start.9 = (bf16[3072,512]{1,0:T(8,128)(2,1)S(1)}, bf16[3072,512]{1,0:T(8,128)(2,1)}, u32[]{:S(2)}) copy-start(bf16[3072,512]{1,0:T(8,128)(2,1)} %copy-done.7) | copy-start | bytes 9437188
  185.8 1.0 copy-start.3
  186.8 40.8 %copy-start.5 = (f32[128,3072]{1,0:T(8,128)}, f32[128,3072]{1,0:T(8,128)S(1)}, u32[]{:S(2)}) copy-start(f32[128,3072]{1,0:T(8,128)S(1)} %get-tuple-element.11) | copy-start | bytes 4718596
  188.6 44.8 %copy-start.10 = (bf16[8,16,768]{2,1,0:T(8,128)(2,1)S(1)}, bf16[8,16,768]{2,1,0:T(8,128)(2,1)}, u32[]{:S(2)}) copy-start(bf16[8,16,768]{2,1,0:T(8,128)(2,1)} %param.9) | copy-start | bytes 589828
  227.6 0.7 copy-start.6
  267.2 1.7 copy-start.2
  268.9 12.6 %copy-start.12 = (bf16[8,16,4,128]{3,2,1,0:T(4,128)(2,1)S(1)}, bf16[8,16,4,128]{3,2,1,0:T(4,128)(2,1)}, u32[]{:S(2)}) copy-start(bf16[8,16,4,128]{3,2,1,0:T(4,128)(2,1)} %copy-done.11) | copy-start | bytes 393220
  272.6 32.9 %copy-start.16 = (f32[512]{0:T(512)S(1)}, f32[512]{0:T(512)}, u32[]{:S(2)}) copy-start(f32[512]{0:T(512)} %copy-done.15) | copy-start | bytes 6148

commit v4 on v3

--- a/solution.py
+++ b/solution.py
@@ -10,6 +10,7 @@
 
 HD = 128
 MB_VOLS = 2
+PARTS = 2
 
 
 beta_one = 0.9
@@ -287,7 +288,7 @@
 
 def gather_kernel(peers, crossing, x_ref, o_ref, *scratch):
     z_send, z_recv, y_send, y_recv, c_send, c_recv = scratch[:6]
-    rows, width = x_ref.shape
+    rows, width = x_ref.shape[0] // PARTS, x_ref.shape[1]
     row, col = lax.axis_index("dp"), lax.axis_index("mp")
     _, across, beside = mesh_partners(peers)
     lines = ({"dp": lax.rem(row + 1, peers)}, {"dp": lax.rem(row + peers - 1, peers)})
@@ -297,9 +298,13 @@
     held = x_ref
     if crossing:
         held, x_send, x_recv = scratch[6:]
-        entering = push(x_ref, held, x_send, x_recv, opposite)
-        entering.start()
-        entering.wait_recv()
+        pieces = [pl.ds(part * rows, rows) for part in range(PARTS)]
+        entering = [
+            push(x_ref.at[piece], held.at[piece], x_send.at[part], x_recv.at[part], opposite)
+            for part, piece in enumerate(pieces)
+        ]
+        for copy in entering:
+            copy.start()
 
     def source_of(side, away):
         return row - away if side == 0 else row + away
@@ -313,82 +318,88 @@
     def slot_of(side, away):
         return 0 if away == 0 else side * (peers - 1) + away
 
-    def place(side, away, owner):
+    def place(part, side, away, owner):
         return o_ref.at[
-            pl.ds(pl.multiple_of(source_of(side, away) * rows, rows), rows),
+            pl.ds(
+                pl.multiple_of((source_of(side, away) * PARTS + part) * rows, rows), rows
+            ),
             pl.ds(pl.multiple_of(owner * width, width), width),
         ]
 
-    def block(side, away):
-        return held if away == 0 else place(side, away, col)
-
-    def onward(side, away):
-        at = side * (peers - 1) + away
-        target = place(side, away, col)
-        return push(block(side, away), target, z_send.at[at], z_recv.at[at], lines[side])
-
-    def sideways(side, away):
-        at = slot_of(side, away)
-        target = place(side, away, col)
-        return push(block(side, away), target, y_send.at[at], y_recv.at[at], across)
-
-    def inward(side, away, both):
-        at = slot_of(side, away) + both * (2 * peers - 1)
-        target = place(side, away, over if both else col)
-        source = target if both else block(side, away)
+    def block(part, side, away):
+        return held.at[pl.ds(part * rows, rows)] if away == 0 else place(part, side, away, col)
+
+    def onward(part, side, away):
+        at = (part * 2 + side) * (peers - 1) + away
+        target = place(part, side, away, col)
+        return push(block(part, side, away), target, z_send.at[at], z_recv.at[at], lines[side])
+
+    def sideways(part, side, away):
+        at = slot_of(side, away) + part * (2 * peers - 1)
+        target = place(part, side, away, col)
+        return push(block(part, side, away), target, y_send.at[at], y_recv.at[at], across)
+
+    def inward(part, side, away, both):
+        at = slot_of(side, away) + (part * 2 + both) * (2 * peers - 1)
+        target = place(part, side, away, over if both else col)
+        source = target if both else block(part, side, away)
         return push(source, target, c_send.at[at], c_recv.at[at], beside)
 
-    every = [(0, 0)] + [(side, away) for away in range(1, peers) for side in (0, 1)]
-
-    def where_there(side, away, action):
+    spots = [(0, 0)] + [(side, away) for away in range(1, peers) for side in (0, 1)]
+    every = [(part, side, away) for side, away in spots for part in range(PARTS)]
+
+    def where_there(part, side, away, action):
         if away == 0:
-            action(side, away)
+            action(part, side, away)
         else:
-            pl.when(there(side, away))(functools.partial(action, side, away))
-
-    def arrive(side, away):
+            pl.when(there(side, away))(functools.partial(action, part, side, away))
+
+    def arrive(part, side, away):
         if away > 0:
-            onward(side, away - 1).wait_recv()
+            onward(part, side, away - 1).wait_recv()
+        elif crossing:
+            entering[part].wait_recv()
         for way in (0, 1) if away == 0 else (side,):
             if away < peers - 1:
-                pl.when(passes(way))(functools.partial(lambda w: onward(w, away).start(), way))
-        sideways(side, away).start()
-        inward(side, away, 0).start()
-
-    def relay(side, away):
-        sideways(side, away).wait_recv()
-        inward(side, away, 1).start()
-
-    def finish(side, away):
-        inward(side, away, 0).wait_recv()
-        inward(side, away, 1).wait_recv()
+                pl.when(passes(way))(functools.partial(lambda w: onward(part, w, away).start(), way))
+        sideways(part, side, away).start()
+        inward(part, side, away, 0).start()
+
+    def relay(part, side, away):
+        sideways(part, side, away).wait_recv()
+        inward(part, side, away, 1).start()
+
+    def finish(part, side, away):
+        inward(part, side, away, 0).wait_recv()
+        inward(part, side, away, 1).wait_recv()
         for way in (0, 1) if away == 0 else (side,):
             if away < peers - 1:
-                pl.when(passes(way))(functools.partial(lambda w: onward(w, away).wait_send(), way))
-        sideways(side, away).wait_send()
-        inward(side, away, 0).wait_send()
-        inward(side, away, 1).wait_send()
-
-    for side, away in every:
-        where_there(side, away, arrive)
-    own_rows = pl.ds(pl.multiple_of(row * rows, rows), rows)
+                pl.when(passes(way))(functools.partial(lambda w: onward(part, w, away).wait_send(), way))
+        sideways(part, side, away).wait_send()
+        inward(part, side, away, 0).wait_send()
+        inward(part, side, away, 1).wait_send()
+
+    for part, side, away in every:
+        where_there(part, side, away, arrive)
+    own_rows = pl.ds(pl.multiple_of(row * PARTS * rows, rows), PARTS * rows)
     o_ref[own_rows, pl.ds(pl.multiple_of(col * width, width), width)] = held[...]
-    for side, away in every:
-        where_there(side, away, relay)
-    for side, away in every:
-        where_there(side, away, finish)
+    for part, side, away in every:
+        where_there(part, side, away, relay)
+    for part, side, away in every:
+        where_there(part, side, away, finish)
     if crossing:
-        entering.wait_send()
+        for copy in entering:
+            copy.wait_send()
 
 
 def gather_tokens(block, crossing=False):
     peers = lax.axis_size("dp")
     shape = (block.shape[0] * peers, block.shape[1] * 4)
     dma = pltpu.SemaphoreType.DMA
-    scratch = [dma((2 * peers - 2,))] * 2 + [dma((2 * peers - 1,))] * 2
-    scratch += [dma((4 * peers - 2,))] * 2
+    scratch = [dma((PARTS * (2 * peers - 2),))] * 2 + [dma((PARTS * (2 * peers - 1),))] * 2
+    scratch += [dma((PARTS * (4 * peers - 2),))] * 2
     if crossing:
-        scratch += [pltpu.VMEM(block.shape, block.dtype), dma, dma]
+        scratch += [pltpu.VMEM(block.shape, block.dtype), dma((PARTS,)), dma((PARTS,))]
     return in_vmem(
         functools.partial(gather_kernel, peers, crossing),
         block,

time: 324 us -> 317 us (0.978)
  Pallas kernels: 242 us -> 236 us
    pallas_call x13, Pallas kernels: 242 us -> 236 us  [in_vmem(): pl.pallas_call(kernel, out_shape=out_shape, in_specs=[pl.BlockSpec(memory...]
where the time goes in v4:
time: 317 us
  Pallas kernels  236 us (74%)
  matrix products  49.5 us (16%)
  local copies, waits for them, and re-layouts  14.9 us (5%)
  other arithmetic  10.2 us (3%)
  blocking collectives  5.06 us (2%)
    pallas_call x13, Pallas kernels, in_vmem(): pl.pallas_call(kernel, out_shape=out_shape, in_specs=[pl.BlockSpec(memory...  236 us
    dot_general x1, matrix products, still_shards(): lax.dot_general(left_side, right_side, (((0,), (0,)), ((), ())), preferre...  17 us
    dot_general x3, matrix products, times_weights(): jnp.dot(left, weights, preferred_element_type=jnp.float32)  7.39 us

profile of v4, /device:TPU:0, one launch (start us, length us, event | category | flops | bytes accessed | tf_op | source)
XLA Modules:
  0.0 316.7 jit_solution(16433137839383068696)
XLA Ops:
  0.7 0.9 dynamic-slice_reduce_fusion
  1.5 0.9 convert_element_type.141
  2.4 2.6 broadcast_select_fusion
  5.0 26.7 %shard_map.94 = bf16[512,3072]{1,0:T(8,128)(2,1)S(1)} custom-call(bf16[128,768]{1,0:T(8,128)(2,1)S(1)} %bitcast.110), custom_call_target="tpu_custom_call" | custom-call | tf_op jit(solution)/shard_map/pallas_call | solution.py:269
  32.3 1.0 fusion.11
  33.7 1.7 copy-done.7
  35.4 1.8 fusion.37.x_ref
  37.2 13.0 %shard_map.95 = bf16[512,512]{1,0:T(8,128)(2,1)S(1)} custom-call(bf16[512,512]{1,0:T(8,128)(2,1)S(1)} %fusion.37.x_ref), custom_call_target="tpu_custom_call" | custom-call | tf_op jit(solution)/shard_map/pallas_call | solution.py:269
  50.4 1.0 fusion.174
  51.9 6.3 %shard_map.96 = bf16[512,512]{1,0:T(8,128)(2,1)S(1)} custom-call(bf16[128,512]{1,0:T(8,128)(2,1)S(1)} %bitcast.108), custom_call_target="tpu_custom_call" | custom-call | tf_op jit(solution)/shard_map/pallas_call | solution.py:269
  58.2 3.7 %convolution_convert_fusion.1.x_ref = bf16[512,3072]{1,0:T(8,128)(2,1)S(1)} fusion(bf16[512,512]{1,0:T(8,128)(2,1)S(1)} %shard_map.96, bf16[3072,512]{1,0:T(8,128)(2,1)} %copy-done.7), kind=kOutput, calls=%fused_computation.28 | convolution fusion | flops 1612185600 | bytes 6815744 | tf_op jit(solution)/shard_map/dot_general | solution.py:659
  62.0 20.1 %shard_map.97.x_ref = bf16[512,768]{1,0:T(8,128)(2,1)S(1)} custom-call(bf16[512,3072]{1,0:T(8,128)(2,1)S(1)} %convolution_convert_fusion.1.x_ref), custom_call_target="tpu_custom_call" | custom-call | tf_op jit(solution)/shard_map/pallas_call | solution.py:269
  82.1 13.9 %shard_map.98 = bf16[128,768]{1,0:T(8,128)(2,1)S(1)} custom-call(bf16[512,768]{1,0:T(8,128)(2,1)S(1)} %shard_map.97.x_ref), custom_call_target="tpu_custom_call" | custom-call | tf_op jit(solution)/shard_map/pallas_call | solution.py:269
  96.1 34.0 %shard_map.99 = bf16[512,3072]{1,0:T(8,128)(2,1)S(1)} custom-call(bf16[128,768]{1,0:T(8,128)(2,1)S(1)} %fusion.73.x_ref), custom_call_target="tpu_custom_call" | custom-call | tf_op jit(solution)/shard_map/pallas_call | solution.py:269
  131.2 1.0 fusion.8
  132.2 1.8 convolution_convert_fusion.3.x_ref
  134.1 13.0 %shard_map.100 = bf16[512,512]{1,0:T(8,128)(2,1)S(1)} custom-call(bf16[512,512]{1,0:T(8,128)(2,1)S(1)} %convolution_convert_fusion.3.x_ref), custom_call_target="tpu_custom_call" | custom-call | tf_op jit(solution)/shard_map/pallas_call | solution.py:269
  147.1 0.7 fusion.172
  147.8 0.9 reshape.142
  148.8 1.6 reshape.141
  151.0 0.9 reshape.143
  152.0 0.9 fusion.85
  152.9 2.5 fusion.179
  155.4 2.0 fusion.57
  157.4 1.0 copy.53
  158.4 2.0 fusion.54
  160.4 1.5 fusion.56
  162.0 2.2 fusion.53
  164.2 1.1 copy.49
  165.4 1.0 copy.56
  166.4 14.0 %shard_map.101 = bf16[512,512]{1,0:T(8,128)(2,1)S(1)} custom-call(bf16[512,512]{1,0:T(8,128)(2,1)S(1)} %pad_maximum_fusion.x_ref), custom_call_target="tpu_custom_call" | custom-call | tf_op jit(solution)/shard_map/pallas_call | solution.py:269
  180.5 0.9 multiply_reduce_fusion
  181.4 1.8 convolution_convert_fusion.x_ref
  183.3 21.2 %shard_map.102.x_ref = bf16[512,768]{1,0:T(8,128)(2,1)S(1)} custom-call(bf16[512,3072]{1,0:T(8,128)(2,1)S(1)} %convolution_convert_fusion.x_ref), custom_call_target="tpu_custom_call" | custom-call | tf_op jit(solution)/shard_map/pallas_call | solution.py:269
  204.5 18.1 %shard_map.103 = bf16[512,768]{1,0:T(8,128)(2,1)S(1)} custom-call(bf16[512,768]{1,0:T(8,128)(2,1)S(1)} %shard_map.102.x_ref), custom_call_target="tpu_custom_call" | custom-call | tf_op jit(solution)/shard_map/pallas_call | solution.py:269
  223.6 5.1 %all-gather.1 = f32[4,2,128]{2,1,0:T(2,128)S(1)} all-gather(f32[1,2,128]{2,1,0:T(2,128)S(1)} %maximum_bitcast_fusion), channel_id=2, replica_groups=mesh['segment'=2,'dp'=4,'mp'=4] {'mp'}, dimensions={0}, use_global_device_ids=true | all-gather | bytes 5120 | tf_op jit(solution)/shard_map/all_gather | solution.py:598
  228.7 1.3 fusion.74.x_ref
  230.0 31.4 %shard_map.104 = bf16[512,3072]{1,0:T(8,128)(2,1)S(1)} custom-call(bf16[128,768]{1,0:T(8,128)(2,1)S(1)} %fusion.74.x_ref), custom_call_target="tpu_custom_call" | custom-call | tf_op jit(solution)/shard_map/pallas_call | solution.py:269
  261.4 1.7 copy-done.2
  263.1 3.7 %convolution_convert_fusion.2.x_ref = bf16[512,512]{1,0:T(8,128)(2,1)S(1)} fusion(bf16[512,3072]{1,0:T(8,128)(2,1)S(1)} %shard_map.104, bf16[3072,512]{1,0:T(8,128)(2,1)} %copy-done.7), kind=kOutput, calls=%fused_computation.50 | convolution fusion | flops 1610874880 | bytes 6815744 | tf_op jit(solution)/shard_map/dot_general | solution.py:655
  266.8 8.2 %shard_map.105 = bf16[128,512]{1,0:T(8,128)(2,1)S(1)} custom-call(bf16[512,512]{1,0:T(8,128)(2,1)S(1)} %convolution_convert_fusion.2.x_ref), custom_call_target="tpu_custom_call" | custom-call | tf_op jit(solution)/shard_map/pallas_call | solution.py:269
  275.7 1.8 fusion.80
  277.5 1.4 fusion.59
  278.9 1.5 fusion.55
  280.5 2.2 fusion.58
  282.7 1.0 copy.63
  283.9 15.8 %shard_map.106 = bf16[512,512]{1,0:T(8,128)(2,1)S(1)} custom-call(bf16[512,512]{1,0:T(8,128)(2,1)S(1)} %pad_maximum_fusion.1.x_ref), custom_call_target="tpu_custom_call" | custom-call | tf_op jit(solution)/shard_map/pallas_call | solution.py:269
  299.7 17.0 %fusion.36 = (f32[1,3072,512]{2,1,0:T(8,128)}, f32[1,3072,512]{2,1,0:T(8,128)}, f32[1,3072,512]{2,1,0:T(8,128)}) fusion(f32[1,3072,512]{2,1,0:T(8,128)} %param.13, f32[1,3072,512]{2,1,0:T(8,128)} %param.12, f32[1,3072,512]{2,1,0:T(8,128)} %param.11, bf16[512,512]{1,0:T(8,128)(2,1)S(1)} %shard_map.106, bf16[512,512]{1,0:T(8,128)(2,1)} %copy-done.3, ...), kind=kOutput, calls=%fused_computation.47 | convolution fusion | flops 1654915072 | bytes 48254976 | tf_op jit(solution)/shard_map/dot_general | solution.py:721
  (75 shorter events, 5.5 us)
Async XLA Ops:
  0.6 32.6 %copy-start.4 = (f32[1,3072,512]{2,1,0:T(8,128)S(1)}, f32[1,3072,512]{2,1,0:T(8,128)}, u32[]{:S(2)}) copy-start(f32[1,3072,512]{2,1,0:T(8,128)} %param.11) | copy-start | bytes 18874372
  31.8 1.9 copy-start
  32.3 3.1 copy-start.17
  33.7 1.7 copy-start.7
  50.3 1.1 copy-start.13
  50.3 1.6 copy-start.14
  50.4 1.5 copy-start.11
  51.4 10.6 %copy-start.18 = (f32[8,4,16]{2,1,0:T(4,128)}, f32[8,4,16]{2,1,0:T(4,128)S(1)}, u32[]{:S(2)}) copy-start(f32[8,4,16]{2,1,0:T(4,128)S(1)} %get-tuple-element.21) | copy-start | bytes 6148
  82.1 50.1 %copy-start.1 = (bf16[512,3072]{1,0:T(8,128)(2,1)S(1)}, bf16[512,3072]{1,0:T(8,128)(2,1)}, u32[]{:S(2)}) copy-start(bf16[512,3072]{1,0:T(8,128)(2,1)} %copy-done) | copy-start | bytes 9437188
  82.1 50.1 %copy-start.8 = (bf16[3072,512]{1,0:T(8,128)(2,1)S(1)}, bf16[3072,512]{1,0:T(8,128)(2,1)}, u32[]{:S(2)}) copy-start(bf16[3072,512]{1,0:T(8,128)(2,1)} %copy-done.7) | copy-start | bytes 9437188
  132.2 1.9 copy-start.15
  164.2 17.2 %copy-start.9 = (bf16[3072,512]{1,0:T(8,128)(2,1)S(1)}, bf16[3072,512]{1,0:T(8,128)(2,1)}, u32[]{:S(2)}) copy-start(bf16[3072,512]{1,0:T(8,128)(2,1)} %copy-done.7) | copy-start | bytes 9437188
  180.5 1.0 copy-start.3
  181.4 41.4 %copy-start.5 = (f32[128,3072]{1,0:T(8,128)}, f32[128,3072]{1,0:T(8,128)S(1)}, u32[]{:S(2)}) copy-start(f32[128,3072]{1,0:T(8,128)S(1)} %get-tuple-element.11) | copy-start | bytes 4718596
  183.3 45.4 %copy-start.10 = (bf16[8,16,768]{2,1,0:T(8,128)(2,1)S(1)}, bf16[8,16,768]{2,1,0:T(8,128)(2,1)}, u32[]{:S(2)}) copy-start(bf16[8,16,768]{2,1,0:T(8,128)(2,1)} %param.9) | copy-start | bytes 589828
  222.8 0.7 copy-start.6
  261.4 1.7 copy-start.2
  263.1 12.6 %copy-start.12 = (bf16[8,16,4,128]{3,2,1,0:T(4,128)(2,1)S(1)}, bf16[8,16,4,128]{3,2,1,0:T(4,128)(2,1)}, u32[]{:S(2)}) copy-start(bf16[8,16,4,128]{3,2,1,0:T(4,128)(2,1)} %copy-done.11) | copy-start | bytes 393220
  266.8 32.9 %copy-start.16 = (f32[512]{0:T(512)S(1)}, f32[512]{0:T(512)}, u32[]{:S(2)}) copy-start(f32[512]{0:T(512)} %copy-done.15) | copy-start | bytes 6148
